TPU v7x, 32 devices: a whole 2x2x4 slice. The times are simulated.
32 devices in a mesh: shot: 2 (over core), strip: 16 (over z, y, x).
Axes of the slice: x: 2, y: 2, z: 4, core: 2. Of those that a mesh axis runs over, the one named last changes fastest.
Arguments:
- source_now: float32 [2, 64, 512, 256], P('shot', None, 'strip'), may hold values from -8 to 8
- source_prev: float32 [2, 64, 512, 256], P('shot', None, 'strip'), may hold values from -8 to 8
- adjoint_now: float32 [2, 64, 512, 256], P('shot', None, 'strip'), may hold values from -8 to 8
- adjoint_prev: float32 [2, 64, 512, 256], P('shot', None, 'strip'), may hold values from -8 to 8
- courant: float32 [512, 256], P('strip'), may hold values from 0.08 to 0.45
- probe_left: float32 [16, 512, 256], P(None, 'strip'), may hold values from -6 to 6
- probe_right: float32 [16, 512, 256], P(None, 'strip'), may hold values from -6 to 6
Outputs:
- left_factor: float32 [16, 512, 256], P(None, 'strip')
- right_factor: float32 [16, 512, 256], P(None, 'strip')
All inputs are finite; a program needn't handle non-finite values.
Results may differ from a plain program's by a relative error of at most 0.0003.
Values sent between devices are 32-bit elements; how exact they have to be, the bound alone decides.
No kernel may reach another device: no remote copies, remote signals or barrier semaphores. Data moves between devices by JAX's collectives and lax.ppermute only.
A program may use at most 64 MiB of HBM per device.

v0:
```python
import math

import jax
import jax.numpy as jnp
from jax import lax
from jax.experimental import pallas as pl
from jax.experimental.pallas import tpu as pltpu
from jax.sharding import PartitionSpec as P

STEPS = 8
LANES = 128
NT = (((1,), (1,)), ((), ()))
MIB = 1 << 20


def in_hbm(x):
    return pltpu.with_memory_space_constraint(x, pltpu.HBM)


def parts_of(x, count):
    parts = []
    for index in range(count):
        part = x.astype(jnp.bfloat16)
        parts.append(part)
        if index + 1 < count:
            x = x - part.astype(jnp.float32)
    return parts


def dot32(a, b, dims):
    return lax.dot_general(a, b, dims, preferred_element_type=jnp.float32)


def call(kernel, outs, vmem_mib, scratch=(), name=None, flops=0, moved=0):
    many = isinstance(outs, (list, tuple))
    spec = pl.BlockSpec(memory_space=pltpu.VMEM)
    return pl.pallas_call(
        kernel,
        out_shape=outs,
        out_specs=[spec] * len(outs) if many else spec,
        scratch_shapes=list(scratch),
        compiler_params=pltpu.CompilerParams(vmem_limit_bytes=vmem_mib * MIB),
        cost_estimate=pl.CostEstimate(flops=flops, bytes_accessed=moved, transcendentals=0),
        name=name,
    )


def f32(*shape):
    return jax.ShapeDtypeStruct(shape, jnp.float32)


def rows_first(x):
    return jnp.concatenate(
        [jnp.swapaxes(x[:, :, t : t + LANES], 0, 1) for t in range(0, x.shape[2], LANES)], 2
    )


def advance_rows(first, last, now, prev, speed, fresh):
    tiles = now.shape[2] // LANES
    spans = [slice(t * LANES, (t + 1) * LANES) for t in range(tiles)]
    lane = lax.broadcasted_iota(jnp.int32, (now.shape[1], LANES), 1)
    at_start, at_end = lane == 0, lane == LANES - 1
    above = [now[first - 1, :, span] for span in spans]
    centre = [now[first, :, span] for span in spans]
    for r in range(first, last):
        below = [now[r + 1, :, span] for span in spans]
        from_left = [pltpu.roll(c, 1, 1) for c in centre]
        from_right = [pltpu.roll(c, LANES - 1, 1) for c in centre]
        for t, span in enumerate(spans):
            left = jnp.where(at_start, from_left[t - 1] if t else 0.0, from_left[t])
            right = jnp.where(at_end, from_right[t + 1] if t + 1 < tiles else 0.0, from_right[t])
            c = speed[r : r + 1, span]
            around = (above[t] + below[t]) + (left + right)
            value = (2.0 - 4.0 * c) * centre[t] + c * around
            if not fresh:
                value = value - prev[r, :, span]
            prev[r, :, span] = value
        above, centre = centre, below


def shards(source_now, source_prev, adjoint_now, adjoint_prev, courant, probe_left, probe_right):
    _, waves, rows, cols = source_now.shape
    rank = probe_left.shape[0]
    strips, shots = lax.axis_size("strip"), lax.axis_size("shot")
    cells = rows * cols
    edge = STEPS
    tall = rows + 2 * edge
    factor_scale = math.sqrt(cells * strips)

    to_other = [(0, 1), (1, 0)]
    to_pair = [(i, i ^ 1) for i in range(strips)]
    to_next = [(i, i + 1) for i in range(1, strips - 1, 2)]
    to_next = to_next + [(b, a) for a, b in to_next]

    def where_am_i():
        return lax.axis_index("shot"), lax.rem(lax.axis_index("strip"), 2) == 0

    def edges_kernel(left, right, speed, pair, other, sem):
        side, even = where_am_i()
        pair_row = jnp.where(even, rows - edge, 0)
        other_row = jnp.where(even, 0, rows - edge)

        def copies(probe):
            made = []
            for index, (out, start) in enumerate(((pair, pair_row), (other, other_row))):
                start = pl.multiple_of(start, 8)
                made.append(
                    pltpu.make_async_copy(
                        probe.at[:, pl.ds(start, edge), :], out.at[pl.ds(0, rank)], sem.at[2 * index]
                    )
                )
                made.append(
                    pltpu.make_async_copy(
                        speed.at[pl.ds(start, edge), :], out.at[rank], sem.at[2 * index + 1]
                    )
                )
            for copy in made:
                copy.start()
            for copy in made:
                copy.wait()

        @pl.when(side == 0)
        def _():
            copies(left)

        @pl.when(side != 0)
        def _():
            copies(right)

    halo = f32(rank + 1, edge, cols)
    far = pl.BlockSpec(memory_space=pltpu.HBM)
    near = pl.BlockSpec(memory_space=pltpu.VMEM)
    pair_edge, other_edge = pl.pallas_call(
        edges_kernel,
        out_shape=[halo, halo],
        in_specs=[far] * 3,
        out_specs=[near] * 2,
        scratch_shapes=[pltpu.SemaphoreType.DMA((4,))],
        compiler_params=pltpu.CompilerParams(vmem_limit_bytes=4 * MIB),
        name="edges",
    )(in_hbm(probe_left), in_hbm(probe_right), in_hbm(courant))
    other_halo = lax.ppermute(other_edge, "strip", to_next)
    pair_halo = lax.ppermute(pair_edge, "strip", to_pair)

    group = math.gcd(waves, 16)

    def split_kernel(
        adjoint_a, adjoint_b, source_a, source_b, left, right, speeds, _,
        out, start, held, probe, speed, sems, sem,
    ):
        side, _ = where_am_i()

        def probe_copy(ref):
            return pltpu.make_async_copy(ref, probe, sem.at[0])

        speed_copy = pltpu.make_async_copy(speeds, speed, sem.at[1])
        speed_copy.start()

        @pl.when(side == 0)
        def _():
            probe_copy(left).start()

        @pl.when(side != 0)
        def _():
            probe_copy(right).start()

        copies = {}
        for index, ref in enumerate((adjoint_a, adjoint_b, source_a, source_b)):
            for first in range(0, waves, group):
                span = pl.ds(first, group)
                copies[index, first] = pltpu.make_async_copy(
                    ref.at[span], held.at[index, span], sems.at[index, first // group]
                )
        for copy in copies.values():
            copy.start()
        for (index, first), copy in copies.items():
            copy.wait()
            for block in range(0, rows, 8):
                for t in range(0, cols, LANES):
                    piece = held[index, first : first + group, block : block + 8, t : t + LANES]
                    high, low = parts_of(jnp.swapaxes(piece, 0, 1), 2)
                    for r in range(8):
                        span = slice((block + r) * cols + t, (block + r) * cols + t + LANES)
                        out[index // 2, index % 2, first : first + group, span] = high[r]
                        out[index // 2, index % 2, waves + first : waves + first + group, span] = low[r]
        speed_copy.wait()
        probe_copy(left).wait()
        for block in range(0, rows, 8):
            span = slice(block, block + 8)
            start[span] = rows_first(probe[:, span, :]) * speed[span, :][:, None, :]

    fields, start = pl.pallas_call(
        split_kernel,
        out_shape=[jax.ShapeDtypeStruct((2, 2, 2 * waves, cells), jnp.bfloat16), f32(rows, rank, cols)],
        in_specs=[far] * 7 + [pl.BlockSpec(memory_space=pl.ANY)],
        out_specs=[near, near],
        scratch_shapes=[
            pltpu.VMEM((4, waves, rows, cols), jnp.float32),
            pltpu.VMEM((rank, rows, cols), jnp.float32),
            pltpu.VMEM((rows, cols), jnp.float32),
            pltpu.SemaphoreType.DMA((4, waves // group)),
            pltpu.SemaphoreType.DMA((2,)),
        ],
        compiler_params=pltpu.CompilerParams(vmem_limit_bytes=24 * MIB),
        cost_estimate=pl.CostEstimate(flops=0, bytes_accessed=16 * waves * cells * 2, transcendentals=0),
        name="split",
    )(
        *map(in_hbm, (adjoint_now[0], adjoint_prev[0], source_now[0], source_prev[0])),
        *map(in_hbm, (probe_left, probe_right, courant)),
        pair_edge,
    )

    def fill_speeds(speeds, speed, above, below):
        speeds[edge : edge + rows, :] = speed[...]
        speeds[:edge, :] = above
        speeds[edge + rows :, :] = below

    def probe_kernel(begin, speed, pair, other, out, now, prev, speeds):
        _, even = where_am_i()
        fill_speeds(
            speeds, speed, jnp.where(even, other[rank], pair[rank]), jnp.where(even, pair[rank], other[rank])
        )
        from_pair = rows_first(pair[:rank] * pair[rank][None])
        from_other = rows_first(other[:rank] * other[rank][None])
        now[:edge] = jnp.where(even, from_other, from_pair)
        now[edge + rows :] = jnp.where(even, from_pair, from_other)
        now[edge : edge + rows] = begin[...]
        a, b = now, prev
        for step in range(1, STEPS + 1):
            advance_rows(step, tall - step, a, b, speeds, step == 1)
            a, b = b, a
        for r in range(rows):
            inverse = 1.0 / speed[r : r + 1, :]
            out[0, :, r * cols : (r + 1) * cols] = a[r + edge] * inverse
            out[1, :, r * cols : (r + 1) * cols] = b[r + edge] * (-inverse)

    state = pltpu.VMEM((tall, rank, cols), jnp.float32)
    probes_own = call(
        probe_kernel,
        f32(2, rank, cells),
        12,
        [state, state, pltpu.VMEM((tall, cols), jnp.float32)],
        name="probes",
    )(start, courant, pair_halo, other_halo)
    probes_other = lax.ppermute(probes_own, "shot", to_other)

    chunk = min(2048, cells)

    def products(fields_ref, probes_ref, side):
        total = jnp.zeros((2 * waves, 2 * rank), jnp.float32)
        for level in range(2):
            for at in range(0, cells, chunk):
                span = slice(at, at + chunk)
                pair = jnp.concatenate(parts_of(probes_ref[level, :, span], 2), 0)
                total = total + dot32(fields_ref[side, level, :, span], pair, NT)
        total = total[:waves] + total[waves:]
        return (total[:, :rank] + total[:, rank:]).T

    def product_kernel(fields_ref, probes_ref, out):
        side, _ = where_am_i()
        out[...] = products(fields_ref, probes_ref, side)

    def product_last_kernel(fields_ref, probes_ref, first_ref, out):
        side, _ = where_am_i()
        mine, theirs = first_ref[...], products(fields_ref, probes_ref, 1 - side)
        both = jnp.concatenate(
            [jnp.where(side == 0, mine, theirs), jnp.where(side == 0, theirs, mine)], 1
        )
        for strip in range(strips):
            out[strip] = both

    flops = 2 * 2 * waves * 2 * rank * cells * 2
    first_product = call(product_kernel, f32(rank, waves), 24, name="product", flops=flops)(
        fields, probes_own
    )
    pieces = call(
        product_last_kernel, f32(strips, rank, 2 * waves), 24, name="product_last", flops=flops
    )(fields, probes_other, first_product)
    pieces = lax.all_to_all(pieces, "strip", 0, 0)

    def combine_kernel(for_own):
        def kernel(pieces_ref, fields_ref, out):
            side, _ = where_am_i()
            side = side if for_own else 1 - side
            weights = jnp.sum(pieces_ref[...], 0)
            weights = jnp.where(side == 0, weights[:, :waves], weights[:, waves:])
            stack = jnp.concatenate(parts_of(weights, 2), 0)
            stack = jnp.concatenate([stack, stack], 1)
            for level in range(2):
                for at in range(0, cells, chunk):
                    span = slice(at, at + chunk)
                    both = jnp.dot(
                        stack,
                        fields_ref[1 - side, level, :, span],
                        preferred_element_type=jnp.float32,
                    )
                    out[level, :, span] = both[:rank] + both[rank:]

        return kernel

    term = f32(2, rank, cells)
    terms_sent = call(combine_kernel(False), term, 24, name="terms_sent", flops=flops)(pieces, fields)
    terms_got = lax.ppermute(terms_sent, "shot", to_other)
    terms_own = call(combine_kernel(True), term, 24, name="terms_own", flops=flops)(pieces, fields)

    def sketch_kernel(own, got, speed, pair, other, out, pair_out, other_out, now, prev, speeds):
        _, even = where_am_i()
        fill_speeds(
            speeds, speed, jnp.where(even, other[rank], pair[rank]), jnp.where(even, pair[rank], other[rank])
        )
        zeros = jnp.zeros((edge, rank, cols), jnp.float32)
        for ref in (now, prev):
            ref[:edge] = zeros
            ref[edge + rows :] = zeros
        for r in range(rows):
            span = slice(r * cols, (r + 1) * cols)
            now[r + edge] = own[0, :, span] + got[0, :, span]
            prev[r + edge] = own[1, :, span] + got[1, :, span]
        a, b = now, prev
        for step in range(1, STEPS + 1):
            reach = min(step, edge - 1)
            advance_rows(edge - reach, edge + rows + reach, a, b, speeds, False)
            if step == edge:
                for r, beside in ((0, 1), (tall - 1, tall - 2)):
                    b[r] = speeds[r : r + 1, :] * a[beside]
            a, b = b, a
        for r in range(rows):
            out[:, r * cols : (r + 1) * cols] = a[r + edge]
        for r in range(edge):
            span = slice(r * cols, (r + 1) * cols)
            above, below = a[r], a[edge + rows + r]
            pair_out[:, span] = jnp.where(even, below, above)
            other_out[:, span] = jnp.where(even, above, below)

    spill = f32(rank, edge * cols)
    sketch_own, pair_spill, other_spill = call(
        sketch_kernel,
        [f32(rank, cells), spill, spill],
        16,
        [state, state, pltpu.VMEM((tall, cols), jnp.float32)],
        name="sketch",
    )(
        terms_own,
        terms_got,
        courant,
        pair_halo,
        other_halo,
    )
    other_add = lax.ppermute(other_spill, "strip", to_next)
    pair_add = lax.ppermute(pair_spill, "strip", to_pair)

    places = shots * strips
    margin = edge * cols

    def gram_kernel(own, pair, other, out, pieces_out):
        _, even = where_am_i()
        top = own[:, :margin] + jnp.where(even, other[...], pair[...])
        bottom = own[:, cells - margin :] + jnp.where(even, pair[...], other[...])
        middle = own[:, margin : cells - margin]
        out[:, :margin] = top
        out[:, margin : cells - margin] = middle
        out[:, cells - margin :] = bottom
        total = jnp.zeros((3 * rank, 3 * rank), jnp.float32)
        for piece in (top, middle, bottom):
            stack = jnp.concatenate(parts_of(piece, 3), 0)
            total = total + dot32(stack, stack, NT)
        wide = total[:, :rank] + total[:, rank : 2 * rank] + total[:, 2 * rank :]
        gram = wide[:rank] + wide[rank : 2 * rank] + wide[2 * rank :]
        half = rank // 2
        gram = jnp.concatenate(
            [gram[:half], gram[half:], jnp.zeros((half, LANES - 2 * rank), jnp.float32)], 1
        )
        for place in range(places):
            pieces_out[place] = gram

    sketch, gram_pieces = call(
        gram_kernel, [f32(rank, cells), f32(places, rank // 2, LANES)], 12, name="gram"
    )(sketch_own, pair_add, other_add)
    sketch_other = lax.ppermute(sketch, "shot", to_other)
    gram_pieces = lax.all_to_all(gram_pieces, ("shot", "strip"), 0, 0)

    def factor_kernel(grams, own, theirs, left_out, right_out):
        side, _ = where_am_i()
        line = lax.broadcasted_iota(jnp.int32, (rank, rank), 0)
        column = lax.broadcasted_iota(jnp.int32, (rank, rank), 1)
        tall_line = lax.broadcasted_iota(jnp.int32, (rank, LANES), 0)
        sides = []
        for shot in range(2):
            halves = jnp.sum(grams[shot * strips : (shot + 1) * strips], 0)
            gram = jnp.concatenate([halves[:, :rank], halves[:, rank : 2 * rank]], 0)
            columns = [jnp.broadcast_to(gram[:, j : j + 1], (rank, LANES)) for j in range(rank)]
            sides.append((columns, [jnp.where(line == column, 1.0, 0.0)]))
        for j in range(rank):
            for columns, inverse in sides:
                factor = columns[j] * (1.0 / columns[j][j : j + 1])
                factor = jnp.where(tall_line > j, factor, 0.0)
                for k in range(j + 1, rank):
                    columns[k] = columns[k] - factor * columns[k][j : j + 1]
                inverse[0] = inverse[0] - factor[:, :rank] * inverse[0][j : j + 1]
        for (columns, inverse), shot, out in zip(sides, (0, 1), (left_out, right_out)):
            pivots = columns[0]
            for j in range(1, rank):
                pivots = jnp.where(tall_line == j, columns[j], pivots)
            inverse = inverse[0] * (lax.rsqrt(pivots[:, :rank]) * factor_scale)
            stack = jnp.concatenate(parts_of(inverse, 3), 0)
            stack = jnp.concatenate([stack] * 3, 1)
            for block in range(0, rows, 8):
                span = slice(block * cols, (block + 8) * cols)
                lines = jnp.where(side == shot, own[:, span], theirs[:, span])
                thick = jnp.concatenate(parts_of(lines, 3), 0)
                solved = jnp.dot(stack, thick, preferred_element_type=jnp.float32)
                solved = solved[:rank] + solved[rank : 2 * rank] + solved[2 * rank :]
                for t in range(0, cols, LANES):
                    tile = [solved[:, r * cols + t : r * cols + t + LANES][None] for r in range(8)]
                    out[:, block : block + 8, t : t + LANES] = jnp.swapaxes(
                        jnp.concatenate(tile, 0), 0, 1
                    )

    factor = f32(rank, rows, cols)
    left_factor, right_factor = call(factor_kernel, [factor, factor], 12, name="factors")(
        gram_pieces, sketch, sketch_other
    )
    return left_factor, right_factor


def solution(mesh):
    return jax.shard_map(
        shards,
        mesh=mesh,
        in_specs=(
            P("shot", None, "strip", None),
            P("shot", None, "strip", None),
            P("shot", None, "strip", None),
            P("shot", None, "strip", None),
            P("strip", None),
            P(None, "strip", None),
            P(None, "strip", None),
        ),
        out_specs=(P(None, "strip", None), P(None, "strip", None)),
        check_vma=False,
    )
```

profile of v0, /device:TPU:0, one launch (start us, length us, event | category | flops | bytes accessed | tf_op | source)
XLA Modules:
  0.0 63.5 jit_solution(3131155470707695738)
XLA Ops:
  0.6 1.0 %edges.1 = (f32[17,8,256]{2,1,0:T(8,128)S(1)}, f32[17,8,256]{2,1,0:T(8,128)S(1)}) custom-call(f32[16,32,256]{2,1,0:T(8,128)} %left.3, f32[16,32,256]{2,1,0:T(8,128)} %right.3, f32[32,256]{1,0:T(8,128)} %speed.5), custom_call_target="tpu_custom_call" | custom-call | tf_op jit(solution)/shard_map/edges/pallas_call | solution.py:133
  1.7 0.7 %collective-permute-start.1 = (f32[17,8,256]{2,1,0:T(8,128)S(1)}, f32[17,8,256]{2,1,0:T(8,128)S(1)}, u32[]{:S(2)}, u32[]{:S(2)}) collective-permute-start(f32[17,8,256]{2,1,0:T(8,128)S(1)} %get-tuple-element.14), channel_id=1, source_target_pairs={{1,2},{3,4},{5,6},{7,8},{9,10},{11,12},{13,14},{2,1},{4,3},{6,5},{... | collective-permute-start | bytes 417800 | tf_op jit(solution)/shard_map/ppermute | solution.py:142
  2.4 5.7 %collective-permute-start = (f32[17,8,256]{2,1,0:T(8,128)S(1)}, f32[17,8,256]{2,1,0:T(8,128)S(1)}, u32[]{:S(2)}, u32[]{:S(2)}) collective-permute-start(f32[17,8,256]{2,1,0:T(8,128)S(1)} %get-tuple-element.11._), channel_id=1, source_target_pairs={{0,1},{1,0},{2,3},{3,2},{4,5},{5,4},{6,7},{7,6},{8,9},{9,8},{10,11... | collective-permute-start | bytes 417800 | tf_op jit(solution)/shard_map/ppermute | solution.py:143
  8.1 0.0 copy-start
  8.1 4.2 %split.1 = (bf16[2,2,128,8192]{3,2,1,0:T(8,128)(2,1)S(1)}, f32[32,16,256]{2,1,0:T(8,128)S(1)}) custom-call(f32[64,32,256]{2,1,0:T(8,128)} %bitcast.4, f32[64,32,256]{2,1,0:T(8,128)} %bitcast.5, f32[64,32,256]{2,1,0:T(8,128)} %bitcast.6, f32[64,32,256]{2,1,0:T(8,128)} %bitcast.7, f32[16,32,256]{2,1,0:T(8,128)} %left.3, f32[16,32,256]{2,1,0:T(8,128)} %right.3, ...), custom_call_target="tpu_custom_call" | custom-call | bytes 16777216 | tf_op jit(solution)/shard_map/split/pallas_call | solution.py:192
  12.3 0.0 collective-permute-done.1.other
  12.3 2.0 %collective-permute-done.pair = f32[17,8,256]{2,1,0:T(8,128)S(1)} collective-permute-done((f32[17,8,256]{2,1,0:T(8,128)S(1)}, f32[17,8,256]{2,1,0:T(8,128)S(1)}, u32[]{:S(2)}, u32[]{:S(2)}) %collective-permute-start) | collective-permute-done | bytes 139296 | tf_op jit(solution)/shard_map/ppermute | solution.py:143
  14.4 0.0 copy-done
  14.4 2.8 %probes.1.probes_ref = f32[2,16,8192]{2,1,0:T(8,128)S(1)} custom-call(f32[32,16,256]{2,1,0:T(8,128)S(1)} %get-tuple-element.13.begin, f32[32,256]{1,0:T(8,128)S(1)} %copy-done, f32[17,8,256]{2,1,0:T(8,128)S(1)} %collective-permute-done.pair, f32[17,8,256]{2,1,0:T(8,128)S(1)} %collective-permute-done.1.other), custom_call_target="tpu_custom_call" | custom-call | tf_op jit(solution)/shard_map/probes/pallas_call | solution.py:238
  17.2 0.1 collective-permute-start.2
  17.3 1.4 %product.1.first_ref = f32[16,64]{1,0:T(8,128)S(1)} custom-call(bf16[2,2,128,8192]{3,2,1,0:T(8,128)(2,1)S(1)} %get-tuple-element.12.fields_ref, f32[2,16,8192]{2,1,0:T(8,128)S(1)} %probes.1.probes_ref), custom_call_target="tpu_custom_call" | custom-call | flops 134217728 | tf_op jit(solution)/shard_map/product/pallas_call | solution.py:273
  18.6 1.3 %collective-permute-done.2.probes_ref = f32[2,16,8192]{2,1,0:T(8,128)S(1)} collective-permute-done((f32[2,16,8192]{2,1,0:T(8,128)S(1)}, f32[2,16,8192]{2,1,0:T(8,128)S(1)}, u32[]{:S(2)}, u32[]{:S(2)}) %collective-permute-start.2) | collective-permute-done | bytes 1048608 | tf_op jit(solution)/shard_map/ppermute | solution.py:245
  19.9 1.4 %product_last.1 = f32[16,16,128]{2,1,0:T(8,128)S(1)} custom-call(bf16[2,2,128,8192]{3,2,1,0:T(8,128)(2,1)S(1)} %get-tuple-element.12.fields_ref, f32[2,16,8192]{2,1,0:T(8,128)S(1)} %collective-permute-done.2.probes_ref, f32[16,64]{1,0:T(8,128)S(1)} %product.1.first_ref), custom_call_target="tpu_custom_call" | custom-call | flops 134217728 | tf_op jit(solution)/shard_map/product_last/pallas_call | solution.py:276
  21.4 13.5 %all_to_all.10.pieces_ref = f32[16,16,128]{2,1,0:T(8,128)S(1)} all-to-all(f32[16,16,128]{2,1,0:T(8,128)S(1)} %product_last.1), channel_id=1, replica_groups=mesh['shot'=2,'strip'=16] {'strip'}, dimensions={0} | all-to-all | bytes 262144 | tf_op jit(solution)/shard_map/all_to_all | solution.py:279
  34.8 0.8 %terms_sent.1 = f32[2,16,8192]{2,1,0:T(8,128)S(1)} custom-call(f32[16,16,128]{2,1,0:T(8,128)S(1)} %all_to_all.10.pieces_ref, bf16[2,2,128,8192]{3,2,1,0:T(8,128)(2,1)S(1)} %get-tuple-element.12.fields_ref), custom_call_target="tpu_custom_call" | custom-call | flops 134217728 | tf_op jit(solution)/shard_map/terms_sent/pallas_call | solution.py:302
  35.7 0.0 collective-permute-start.3
  35.7 0.8 %terms_own.1.own = f32[2,16,8192]{2,1,0:T(8,128)S(1)} custom-call(f32[16,16,128]{2,1,0:T(8,128)S(1)} %all_to_all.10.pieces_ref, bf16[2,2,128,8192]{3,2,1,0:T(8,128)(2,1)S(1)} %get-tuple-element.12.fields_ref), custom_call_target="tpu_custom_call" | custom-call | flops 134217728 | tf_op jit(solution)/shard_map/terms_own/pallas_call | solution.py:304
  36.6 1.8 %collective-permute-done.3.got = f32[2,16,8192]{2,1,0:T(8,128)S(1)} collective-permute-done((f32[2,16,8192]{2,1,0:T(8,128)S(1)}, f32[2,16,8192]{2,1,0:T(8,128)S(1)}, u32[]{:S(2)}, u32[]{:S(2)}) %collective-permute-start.3) | collective-permute-done | bytes 1048608 | tf_op jit(solution)/shard_map/ppermute | solution.py:303
  38.4 2.8 %sketch.1 = (f32[16,8192]{1,0:T(8,128)S(1)}, f32[16,2048]{1,0:T(8,128)S(1)}, f32[16,2048]{1,0:T(8,128)S(1)}) custom-call(f32[2,16,8192]{2,1,0:T(8,128)S(1)} %terms_own.1.own, f32[2,16,8192]{2,1,0:T(8,128)S(1)} %collective-permute-done.3.got, f32[32,256]{1,0:T(8,128)S(1)} %copy-done, f32[17,8,256]{2,1,0:T(8,128)S(1)} %collective-permute-done.pair, ...), custom_call_target="tpu_custom_call" | custom-call | tf_op jit(solution)/shard_map/sketch/pallas_call | solution.py:336
  41.2 1.2 %collective-permute-start.4 = (f32[16,2048]{1,0:T(8,128)S(1)}, f32[16,2048]{1,0:T(8,128)S(1)}, u32[]{:S(2)}, u32[]{:S(2)}) collective-permute-start(f32[16,2048]{1,0:T(8,128)S(1)} %get-tuple-element.16), channel_id=1, source_target_pairs={{0,1},{1,0},{2,3},{3,2},{4,5},{5,4},{6,7},{7,6},{8,9},{9,8},{10,11... | collective-permute-start | bytes 393224 | tf_op jit(solution)/shard_map/ppermute | solution.py:350
  42.3 0.7 %collective-permute-start.5 = (f32[16,2048]{1,0:T(8,128)S(1)}, f32[16,2048]{1,0:T(8,128)S(1)}, u32[]{:S(2)}, u32[]{:S(2)}) collective-permute-start(f32[16,2048]{1,0:T(8,128)S(1)} %get-tuple-element.17), channel_id=1, source_target_pairs={{1,2},{3,4},{5,6},{7,8},{9,10},{11,12},{13,14},{2,1},{4,3},{6,5},{... | collective-permute-start | bytes 393224 | tf_op jit(solution)/shard_map/ppermute | solution.py:349
  43.0 4.2 %collective-permute-done.4.pair = f32[16,2048]{1,0:T(8,128)S(1)} collective-permute-done((f32[16,2048]{1,0:T(8,128)S(1)}, f32[16,2048]{1,0:T(8,128)S(1)}, u32[]{:S(2)}, u32[]{:S(2)}) %collective-permute-start.4) | collective-permute-done | bytes 131104 | tf_op jit(solution)/shard_map/ppermute | solution.py:350
  47.2 0.0 collective-permute-done.5.other
  47.2 0.5 gram.1
  47.7 0.1 collective-permute-start.6
  47.8 13.7 %all_to_all.11.grams = f32[32,8,128]{2,1,0:T(8,128)S(1)} all-to-all(f32[32,8,128]{2,1,0:T(8,128)S(1)} %get-tuple-element.18), channel_id=1, replica_groups=mesh['shot'=2,'strip'=16] {'shot','strip'}, dimensions={0} | all-to-all | bytes 262144 | tf_op jit(solution)/shard_map/all_to_all | solution.py:380
  61.5 0.0 collective-permute-done.6.theirs
  61.5 2.0 %factors.1 = (f32[16,32,256]{2,1,0:T(8,128)}, f32[16,32,256]{2,1,0:T(8,128)}) custom-call(f32[32,8,128]{2,1,0:T(8,128)S(1)} %all_to_all.11.grams, f32[16,8192]{1,0:T(8,128)S(1)} %get-tuple-element.19.own, f32[16,8192]{1,0:T(8,128)S(1)} %collective-permute-done.6.theirs), custom_call_target="tpu_custom_call" | custom-call | tf_op jit(solution)/shard_map/factors/pallas_call | solution.py:420
Async XLA Ops:
  1.7 10.7 %collective-permute-start.1 = (f32[17,8,256]{2,1,0:T(8,128)S(1)}, f32[17,8,256]{2,1,0:T(8,128)S(1)}, u32[]{:S(2)}, u32[]{:S(2)}) collective-permute-start(f32[17,8,256]{2,1,0:T(8,128)S(1)} %get-tuple-element.14), channel_id=1, source_target_pairs={{1,2},{3,4},{5,6},{7,8},{9,10},{11,12},{13,14},{2,1},{4,3},{6,5},{... | collective-permute-start | bytes 417800 | tf_op jit(solution)/shard_map/ppermute | solution.py:142
  2.4 12.0 %collective-permute-start = (f32[17,8,256]{2,1,0:T(8,128)S(1)}, f32[17,8,256]{2,1,0:T(8,128)S(1)}, u32[]{:S(2)}, u32[]{:S(2)}) collective-permute-start(f32[17,8,256]{2,1,0:T(8,128)S(1)} %get-tuple-element.11._), channel_id=1, source_target_pairs={{0,1},{1,0},{2,3},{3,2},{4,5},{5,4},{6,7},{7,6},{8,9},{9,8},{10,11... | collective-permute-start | bytes 417800 | tf_op jit(solution)/shard_map/ppermute | solution.py:143
  8.1 6.3 %copy-start = (f32[32,256]{1,0:T(8,128)S(1)}, f32[32,256]{1,0:T(8,128)}, u32[]{:S(2)}) copy-start(f32[32,256]{1,0:T(8,128)} %speed.5) | copy-start | bytes 98308
  17.2 2.7 %collective-permute-start.2 = (f32[2,16,8192]{2,1,0:T(8,128)S(1)}, f32[2,16,8192]{2,1,0:T(8,128)S(1)}, u32[]{:S(2)}, u32[]{:S(2)}) collective-permute-start(f32[2,16,8192]{2,1,0:T(8,128)S(1)} %probes.1.probes_ref), channel_id=1, source_target_pairs={{0,16},{16,0},{1,17},{17,1},{2,18},{18,2},{3,19},{19,3},{4,20},{20... | collective-permute-start | bytes 3145736 | tf_op jit(solution)/shard_map/ppermute | solution.py:245
  35.7 2.7 %collective-permute-start.3 = (f32[2,16,8192]{2,1,0:T(8,128)S(1)}, f32[2,16,8192]{2,1,0:T(8,128)S(1)}, u32[]{:S(2)}, u32[]{:S(2)}) collective-permute-start(f32[2,16,8192]{2,1,0:T(8,128)S(1)} %terms_sent.1), channel_id=1, source_target_pairs={{0,16},{16,0},{1,17},{17,1},{2,18},{18,2},{3,19},{19,3},{4,20},{20... | collective-permute-start | bytes 3145736 | tf_op jit(solution)/shard_map/ppermute | solution.py:303
  41.2 6.0 %collective-permute-start.4 = (f32[16,2048]{1,0:T(8,128)S(1)}, f32[16,2048]{1,0:T(8,128)S(1)}, u32[]{:S(2)}, u32[]{:S(2)}) collective-permute-start(f32[16,2048]{1,0:T(8,128)S(1)} %get-tuple-element.16), channel_id=1, source_target_pairs={{0,1},{1,0},{2,3},{3,2},{4,5},{5,4},{6,7},{7,6},{8,9},{9,8},{10,11... | collective-permute-start | bytes 393224 | tf_op jit(solution)/shard_map/ppermute | solution.py:350
  42.3 4.9 %collective-permute-start.5 = (f32[16,2048]{1,0:T(8,128)S(1)}, f32[16,2048]{1,0:T(8,128)S(1)}, u32[]{:S(2)}, u32[]{:S(2)}) collective-permute-start(f32[16,2048]{1,0:T(8,128)S(1)} %get-tuple-element.17), channel_id=1, source_target_pairs={{1,2},{3,4},{5,6},{7,8},{9,10},{11,12},{13,14},{2,1},{4,3},{6,5},{... | collective-permute-start | bytes 393224 | tf_op jit(solution)/shard_map/ppermute | solution.py:349
  47.7 13.8 %collective-permute-start.6 = (f32[16,8192]{1,0:T(8,128)S(1)}, f32[16,8192]{1,0:T(8,128)S(1)}, u32[]{:S(2)}, u32[]{:S(2)}) collective-permute-start(f32[16,8192]{1,0:T(8,128)S(1)} %get-tuple-element.19.own), channel_id=1, source_target_pairs={{0,16},{16,0},{1,17},{17,1},{2,18},{18,2},{3,19},{19,3},{4,20},{20... | collective-permute-start | bytes 1572872 | tf_op jit(solution)/shard_map/ppermute | solution.py:379
where the time goes:
time: 63.7 us; the launch traced here: 63.5 us
  blocking collectives  27.2 us (43%)
  Pallas kernels  17.9 us (28%)
  waiting for transfers between devices  9.32 us (15%)
  starting transfers between devices  8.4 us (13%)
  between operations  0.73 us (1%)
    all_to_all x1, blocking collectives, shards(): gram_pieces = lax.all_to_all(gram_pieces, ('shot', 'strip'), 0, 0)  13.7 us
    all_to_all x1, blocking collectives, shards(): pieces = lax.all_to_all(pieces, 'strip', 0, 0)  13.5 us
    ppermute x1, starting transfers between devices, shards(): pair_halo = lax.ppermute(pair_edge, 'strip', to_pair)  5.73 us
    pallas_call x1, Pallas kernels, shards(): pl.pallas_call(split_kernel, out_shape=[jax.ShapeDtypeStruct((2, 2, 2 * w...  4.24 us
    ppermute x1, waiting for transfers between devices, shards(): pair_add = lax.ppermute(pair_spill, 'strip', to_pair)  4.19 us
    pallas_call x1, Pallas kernels, shards(): call(probe_kernel, f32(2, rank, cells), 12, [state, state, pltpu.VMEM((ta...  2.82 us
    pallas_call x1, Pallas kernels, shards(): call(sketch_kernel, [f32(rank, cells), spill, spill], 16, [state, state,...  2.81 us
    ppermute x1, waiting for transfers between devices, shards(): pair_halo = lax.ppermute(pair_edge, 'strip', to_pair)  2.03 us
  transfers between devices with their start and end apart: 7, of which 4 were waited for; matrix products, arithmetic and copies ran while one was open for 0% of the time, Pallas kernels for 10%

commit v1 on v0

v1 whole, which is shorter than its diff:
```python
import math

import jax
import jax.numpy as jnp
from jax import lax
from jax.experimental import pallas as pl
from jax.experimental.pallas import tpu as pltpu
from jax.sharding import PartitionSpec as P

STEPS = 8
LANES = 128
NT = (((1,), (1,)), ((), ()))
MIB = 1 << 20


def in_hbm(x):
    return pltpu.with_memory_space_constraint(x, pltpu.HBM)


def parts_of(x, count):
    parts = []
    for index in range(count):
        part = x.astype(jnp.bfloat16)
        parts.append(part)
        if index + 1 < count:
            x = x - part.astype(jnp.float32)
    return parts


def dot32(a, b, dims):
    return lax.dot_general(a, b, dims, preferred_element_type=jnp.float32)


def call(kernel, outs, vmem_mib, scratch=(), name=None, flops=0, moved=0):
    many = isinstance(outs, (list, tuple))
    spec = pl.BlockSpec(memory_space=pltpu.VMEM)
    return pl.pallas_call(
        kernel,
        out_shape=outs,
        out_specs=[spec] * len(outs) if many else spec,
        scratch_shapes=list(scratch),
        compiler_params=pltpu.CompilerParams(vmem_limit_bytes=vmem_mib * MIB),
        cost_estimate=pl.CostEstimate(flops=flops, bytes_accessed=moved, transcendentals=0),
        name=name,
    )


def f32(*shape):
    return jax.ShapeDtypeStruct(shape, jnp.float32)


def rows_first(x):
    return jnp.concatenate(
        [jnp.swapaxes(x[:, :, t : t + LANES], 0, 1) for t in range(0, x.shape[2], LANES)], 2
    )


def advance_rows(first, last, now, prev, speed, fresh):
    tiles = now.shape[2] // LANES
    spans = [slice(t * LANES, (t + 1) * LANES) for t in range(tiles)]
    lane = lax.broadcasted_iota(jnp.int32, (now.shape[1], LANES), 1)
    at_start, at_end = lane == 0, lane == LANES - 1
    above = [now[first - 1, :, span] for span in spans]
    centre = [now[first, :, span] for span in spans]
    for r in range(first, last):
        below = [now[r + 1, :, span] for span in spans]
        from_left = [pltpu.roll(c, 1, 1) for c in centre]
        from_right = [pltpu.roll(c, LANES - 1, 1) for c in centre]
        for t, span in enumerate(spans):
            left = jnp.where(at_start, from_left[t - 1] if t else 0.0, from_left[t])
            right = jnp.where(at_end, from_right[t + 1] if t + 1 < tiles else 0.0, from_right[t])
            c = speed[r : r + 1, span]
            around = (above[t] + below[t]) + (left + right)
            value = (2.0 - 4.0 * c) * centre[t] + c * around
            if not fresh:
                value = value - prev[r, :, span]
            prev[r, :, span] = value
        above, centre = centre, below


def shards(source_now, source_prev, adjoint_now, adjoint_prev, courant, probe_left, probe_right):
    _, waves, rows, cols = source_now.shape
    rank = probe_left.shape[0]
    strips, shots = lax.axis_size("strip"), lax.axis_size("shot")
    cells = rows * cols
    edge = STEPS
    factor_scale = math.sqrt(cells * strips)

    to_other = [(0, 1), (1, 0)]
    to_pair = [(i, i ^ 1) for i in range(strips)]
    to_next = [(i, i + 1) for i in range(1, strips - 1, 2)]
    to_next = to_next + [(b, a) for a, b in to_next]

    def where_am_i():
        return lax.axis_index("shot"), lax.rem(lax.axis_index("strip"), 2) == 0

    def edges_kernel(left, right, speed, pair, other, sem):
        side, even = where_am_i()
        pair_row = jnp.where(even, rows - edge, 0)
        other_row = jnp.where(even, 0, rows - edge)

        def copies(probe):
            made = []
            for index, (out, start) in enumerate(((pair, pair_row), (other, other_row))):
                start = pl.multiple_of(start, 8)
                made.append(
                    pltpu.make_async_copy(
                        probe.at[:, pl.ds(start, edge), :], out.at[pl.ds(0, rank)], sem.at[2 * index]
                    )
                )
                made.append(
                    pltpu.make_async_copy(
                        speed.at[pl.ds(start, edge), :], out.at[rank], sem.at[2 * index + 1]
                    )
                )
            for copy in made:
                copy.start()
            for copy in made:
                copy.wait()

        @pl.when(side == 0)
        def _():
            copies(left)

        @pl.when(side != 0)
        def _():
            copies(right)

    halo = f32(rank + 1, edge, cols)
    far = pl.BlockSpec(memory_space=pltpu.HBM)
    near = pl.BlockSpec(memory_space=pltpu.VMEM)
    pair_edge, other_edge = pl.pallas_call(
        edges_kernel,
        out_shape=[halo, halo],
        in_specs=[far] * 3,
        out_specs=[near] * 2,
        scratch_shapes=[pltpu.SemaphoreType.DMA((4,))],
        compiler_params=pltpu.CompilerParams(vmem_limit_bytes=4 * MIB),
        cost_estimate=pl.CostEstimate(flops=20000000000, bytes_accessed=4194304, transcendentals=0),
        name="edges",
    )(in_hbm(probe_left), in_hbm(probe_right), in_hbm(courant))
    other_halo = lax.ppermute(other_edge, "strip", to_next)
    pair_halo = lax.ppermute(pair_edge, "strip", to_pair)

    group = math.gcd(waves, 16)

    def lay_out(piece, out, high_at, low_at, at, t):
        high, low = parts_of(jnp.swapaxes(piece, 0, 1), 2)
        for r in range(8):
            span = slice((at + r) * cols + t, (at + r) * cols + t + LANES)
            out[high_at, span] = high[r]
            out[low_at, span] = low[r]

    def split_kernel(
        adjoint_a, adjoint_b, source_a, source_b, left, right, speeds, _,
        out, start, inner_stage, probe, speed, sem,
    ):
        side, _ = where_am_i()

        def probe_copy(ref):
            return pltpu.make_async_copy(ref, probe, sem.at[0])

        speed_copy = pltpu.make_async_copy(speeds, speed, sem.at[1])
        speed_copy.start()

        @pl.when(side == 0)
        def _():
            probe_copy(left).start()

        @pl.when(side != 0)
        def _():
            probe_copy(right).start()

        for level, adjoint, source in ((0, adjoint_a, source_a), (1, adjoint_b, source_b)):
            for first in range(0, waves, group):
                some = slice(first, first + group)
                low = slice(waves + first, waves + first + group)
                for block in range(0, rows, 8):
                    for t in range(0, cols, LANES):
                        span = slice(t, t + LANES)
                        mine, other = adjoint[some, block : block + 8, span], source[some, block : block + 8, span]
                        if edge <= block < rows - edge:
                            sent = jnp.where(side == 0, mine, other)
                            inner_stage[level, some, block - edge : block - edge + 8, span] = sent
                        lay_out(mine, out.at[0, level], some, low, block, t)
                        lay_out(other, out.at[1, level], some, low, block, t)
        speed_copy.wait()
        probe_copy(left).wait()
        for block in range(0, rows, 8):
            span = slice(block, block + 8)
            start[span] = rows_first(probe[:, span, :]) * speed[span, :][:, None, :]

    def stage_kernel(adjoint_a, adjoint_b, source_a, source_b, _, out):
        side, _ = where_am_i()

        def stage(pair):
            for level, ref in enumerate(pair):
                out[level, :, :edge] = ref[:, :edge]
                out[level, :, edge:] = ref[:, rows - edge :]

        @pl.when(side == 0)
        def _():
            stage((adjoint_a, adjoint_b))

        @pl.when(side != 0)
        def _():
            stage((source_a, source_b))

    kinds = (adjoint_now[0], adjoint_prev[0], source_now[0], source_prev[0])
    rim_stage = pl.pallas_call(
        stage_kernel,
        out_shape=f32(2, waves, 2 * edge, cols),
        in_specs=[near] * 4 + [pl.BlockSpec(memory_space=pl.ANY)],
        out_specs=near,
        compiler_params=pltpu.CompilerParams(vmem_limit_bytes=26 * MIB),
        name="stage",
    )(*kinds, pair_edge)
    fields, start, inner_stage = pl.pallas_call(
        split_kernel,
        out_shape=[
            jax.ShapeDtypeStruct((2, 2, 2 * waves, cells), jnp.bfloat16),
            f32(rows, rank, cols),
            f32(2, waves, rows - 2 * edge, cols),
        ],
        in_specs=[near] * 4 + [far] * 3 + [pl.BlockSpec(memory_space=pl.ANY)],
        out_specs=[near] * 3,
        scratch_shapes=[
            pltpu.VMEM((rank, rows, cols), jnp.float32),
            pltpu.VMEM((rows, cols), jnp.float32),
            pltpu.SemaphoreType.DMA((2,)),
        ],
        compiler_params=pltpu.CompilerParams(vmem_limit_bytes=26 * MIB),
        cost_estimate=pl.CostEstimate(flops=0, bytes_accessed=16 * waves * cells * 2, transcendentals=0),
        name="split",
    )(
        *kinds,
        *map(in_hbm, (probe_left, probe_right, courant)),
        pair_edge,
    )
    rim_raw = lax.ppermute(rim_stage, "shot", to_other)

    inner = rows - 2 * edge
    rim = edge * cols

    def inner_kernel(begin, speed, out, saved, now, prev):
        now[...] = begin[...]
        a, b = now, prev
        for step in range(STEPS):
            saved[step, :2] = a[step : step + 2]
            saved[step, 2:] = a[rows - 2 - step : rows - step]
            advance_rows(step + 1, rows - 1 - step, a, b, speed, step == 0)
            a, b = b, a
        for r in range(edge, edge + inner):
            span = slice((r - edge) * cols, (r - edge + 1) * cols)
            inverse = 1.0 / speed[r : r + 1, :]
            out[0, :, span] = a[r] * inverse
            out[1, :, span] = b[r] * (-inverse)

    state = pltpu.VMEM((rows, rank, cols), jnp.float32)
    inner_own, saved = call(
        inner_kernel,
        [f32(2, rank, inner * cols), f32(STEPS, 4, rank, cols)],
        12,
        [state, state],
        name="probes_inner",
    )(start, courant)
    inner_other = lax.ppermute(inner_own, "shot", to_other)

    def far_speeds(pair, other):
        _, even = where_am_i()
        above = jnp.where(even, other[rank], pair[rank])
        below = jnp.where(even, pair[rank], other[rank])
        return above, below

    def rim_kernel(saved, speed, pair, other, out, up_now, up_prev, low_now, low_prev, up_speed, low_speed):
        _, even = where_am_i()
        up_speed[:edge, :], low_speed[edge + 1 :, :] = far_speeds(pair, other)
        up_speed[edge : 2 * edge, :] = speed[:edge, :]
        low_speed[1 : edge + 1, :] = speed[rows - edge :, :]
        from_pair = rows_first(pair[:rank] * pair[rank][None])
        from_other = rows_first(other[:rank] * other[rank][None])
        up_now[:edge] = jnp.where(even, from_other, from_pair)
        low_now[edge + 1 :] = jnp.where(even, from_pair, from_other)
        up_now[edge : edge + 2] = saved[0, :2]
        low_now[edge - 1 : edge + 1] = saved[0, 2:]
        a, b, c, d = up_now, up_prev, low_now, low_prev
        for step in range(1, STEPS + 1):
            advance_rows(step, edge + step, a, b, up_speed, step == 1)
            advance_rows(edge + 1 - step, 2 * edge + 1 - step, c, d, low_speed, step == 1)
            if step < STEPS:
                b[edge + step : edge + step + 2] = saved[step, :2]
                d[edge - 1 - step : edge + 1 - step] = saved[step, 2:]
            a, b, c, d = b, a, d, c
        for r in range(edge):
            upper = slice(r * cols, (r + 1) * cols)
            lower = slice(rim + r * cols, rim + (r + 1) * cols)
            inverse = 1.0 / speed[r : r + 1, :]
            out[0, :, upper] = a[edge + r] * inverse
            out[1, :, upper] = b[edge + r] * (-inverse)
            inverse = 1.0 / speed[rows - edge + r : rows - edge + r + 1, :]
            out[0, :, lower] = c[r + 1] * inverse
            out[1, :, lower] = d[r + 1] * (-inverse)

    short = pltpu.VMEM((2 * edge + 1, rank, cols), jnp.float32)
    short_speed = pltpu.VMEM((2 * edge + 1, cols), jnp.float32)
    rim_own = call(
        rim_kernel,
        f32(2, rank, 2 * rim),
        12,
        [short] * 4 + [short_speed] * 2,
        name="probes_rim",
    )(saved, courant, pair_halo, other_halo)
    rim_other = lax.ppermute(rim_own, "shot", to_other)

    def products(fields_ref, probes_ref, side, inside):
        total = jnp.zeros((2 * waves, 2 * rank), jnp.float32)
        places = [(rim, 0, inner * cols)] if inside else [(0, 0, rim), (cells - rim, rim, rim)]
        for level in range(2):
            for at, probe_at, count in places:
                pair = jnp.concatenate(parts_of(probes_ref[level, :, probe_at : probe_at + count], 2), 0)
                total = total + dot32(fields_ref[side, level, :, at : at + count], pair, NT)
        total = total[:waves] + total[waves:]
        return (total[:, :rank] + total[:, rank:]).T

    def product_kernel(fields_ref, inner_mine, inner_theirs, rim_mine, raw, mine, theirs, swapped):
        side, _ = where_am_i()
        mine[...] = products(fields_ref, inner_mine, side, True) + products(
            fields_ref, rim_mine, side, False
        )
        theirs[...] = products(fields_ref, inner_theirs, 1 - side, True)
        lay_out_raw(raw, swapped)

    def lay_out_raw(raw, out):
        for level in range(2):
            for first in range(0, waves, group):
                some = slice(first, first + group)
                low = slice(waves + first, waves + first + group)
                for block in range(0, raw.shape[2], 8):
                    for t in range(0, cols, LANES):
                        piece = raw[level, some, block : block + 8, t : t + LANES]
                        lay_out(piece, out.at[level], some, low, block, t)

    half = rank // 2

    def product_last_kernel(fields_ref, rim_theirs, mine_ref, theirs_ref, out):
        side, _ = where_am_i()
        mine = mine_ref[...]
        theirs = theirs_ref[...] + products(fields_ref, rim_theirs, 1 - side, False)
        for shot in range(shots):
            weights = jnp.where(side == shot, mine, theirs)
            weights = jnp.concatenate([weights[:half], weights[half:]], 1)
            for strip in range(strips):
                out[shot * strips + strip] = weights

    flops = 2 * 2 * waves * 2 * rank * cells * 2
    mine, theirs, rim_swapped = call(
        product_kernel,
        [f32(rank, waves)] * 2 + [jax.ShapeDtypeStruct((2, 2 * waves, 2 * rim), jnp.bfloat16)],
        24,
        name="product",
    )(fields, inner_own, inner_other, rim_own, rim_raw)
    pieces = call(
        product_last_kernel, f32(shots * strips, half, 2 * waves), 24, name="product_last"
    )(fields, rim_other, mine, theirs)
    inner_stage, pieces = lax.optimization_barrier((inner_stage, pieces))
    inner_raw = lax.ppermute(inner_stage, "shot", to_other)
    pieces = lax.all_to_all(pieces, ("shot", "strip"), 0, 0)

    def combine(pieces_ref, fields_ref, swapped_ref, places, out):
        side, _ = where_am_i()
        weights = []
        for shot in range(shots):
            packed = jnp.sum(pieces_ref[shot * strips : (shot + 1) * strips], 0)
            weights.append(jnp.concatenate([packed[:, :waves], packed[:, waves:]], 0))
        stacks = []
        for own, other in (weights, weights[::-1]):
            stack = jnp.concatenate(parts_of(jnp.where(side == 0, own, other), 2), 0)
            stacks.append(jnp.concatenate([stack, stack], 1))
        for level in range(2):
            for at, place, count in places:
                both = jnp.dot(
                    stacks[0],
                    fields_ref[1 - side, level, :, at : at + count],
                    preferred_element_type=jnp.float32,
                ) + jnp.dot(
                    stacks[1],
                    swapped_ref[level, :, place : place + count],
                    preferred_element_type=jnp.float32,
                )
                out[level, :, place : place + count] = both[:rank] + both[rank:]

    def rim_terms_kernel(pieces_ref, fields_ref, swapped_ref, out):
        places = [(0, 0, rim), (cells - rim, rim, rim)]
        combine(pieces_ref, fields_ref, swapped_ref, places, out)

    def inner_terms_kernel(pieces_ref, fields_ref, raw, _, out, swapped):
        lay_out_raw(raw, swapped)
        combine(pieces_ref, fields_ref, swapped, [(rim, 0, inner * cols)], out)

    rim_terms = call(
        rim_terms_kernel, f32(2, rank, 2 * rim), 24, name="terms_rim", flops=flops
    )(pieces, fields, rim_swapped)

    def spill_kernel(
        own, speed, pair, other, pair_out, other_out,
        up_now, up_prev, low_now, low_prev, up_speed, low_speed,
    ):
        _, even = where_am_i()
        above, below = far_speeds(pair, other)
        up_speed[1 : edge + 1, :] = above
        up_speed[edge + 1 :, :] = speed[:edge, :]
        low_speed[:edge, :] = speed[rows - edge :, :]
        low_speed[edge : 2 * edge, :] = below
        zeros = jnp.zeros((edge + 1, rank, cols), jnp.float32)
        for up, low, level in ((up_now, low_now, 0), (up_prev, low_prev, 1)):
            up[: edge + 1] = zeros
            low[edge:] = zeros
            for r in range(edge):
                span = slice(r * cols, (r + 1) * cols)
                up[edge + 1 + r] = own[level, :, span]
                span = slice(rim + r * cols, rim + (r + 1) * cols)
                low[r] = own[level, :, span]
        a, b, c, d = up_now, up_prev, low_now, low_prev
        for step in range(1, STEPS + 1):
            advance_rows(edge + 1 - step, 2 * edge + 1 - step, a, b, up_speed, False)
            advance_rows(step, edge + step, c, d, low_speed, False)
            a, b, c, d = b, a, d, c
        for r in range(edge):
            span = slice(r * cols, (r + 1) * cols)
            upper, lower = a[1 + r], c[edge + r]
            pair_out[:, span] = jnp.where(even, lower, upper)
            other_out[:, span] = jnp.where(even, upper, lower)

    spill = f32(rank, rim)
    pair_spill, other_spill = call(
        spill_kernel,
        [spill, spill],
        16,
        [short] * 4 + [short_speed] * 2,
        name="spill",
    )(rim_terms, courant, pair_halo, other_halo)
    other_add = lax.ppermute(other_spill, "strip", to_next)
    pair_add = lax.ppermute(pair_spill, "strip", to_pair)

    inner_terms = call(
        inner_terms_kernel,
        f32(2, rank, inner * cols),
        24,
        [pltpu.VMEM((2, 2 * waves, inner * cols), jnp.bfloat16)],
        name="terms_inner",
        flops=flops,
    )(pieces, fields, inner_raw, pair_spill)
    pad = STEPS // 2 + 1
    tall = rows + 2 * pad

    def sketch_kernel(
        rim_part, inner_part, speed, pair, other, _, out, now, prev, speeds
    ):
        above, below = far_speeds(pair, other)
        speeds[:pad, :] = above[edge - pad :, :]
        speeds[pad : pad + rows, :] = speed[...]
        speeds[pad + rows :, :] = below[:pad, :]
        zeros = jnp.zeros((pad, rank, cols), jnp.float32)
        for ref in (now, prev):
            ref[:pad] = zeros
            ref[pad + rows :] = zeros
        for r in range(rows):
            part, line = rim_part, r
            if edge <= r < rows - edge:
                part, line = inner_part, r - edge
            elif r >= edge:
                line = r - inner
            span = slice(line * cols, (line + 1) * cols)
            now[r + pad] = part[0, :, span]
            prev[r + pad] = part[1, :, span]
        a, b = now, prev
        for step in range(1, STEPS + 1):
            reach = min(step, STEPS - step)
            advance_rows(pad - reach, pad + rows + reach, a, b, speeds, False)
            a, b = b, a
        for r in range(rows):
            out[:, r * cols : (r + 1) * cols] = a[r + pad]

    lines = pltpu.VMEM((tall, rank, cols), jnp.float32)
    sketch_own = call(
        sketch_kernel,
        f32(rank, cells),
        16,
        [lines, lines, pltpu.VMEM((tall, cols), jnp.float32)],
        name="sketch",
        moved=8 * MIB,
    )(rim_terms, inner_terms, courant, pair_halo, other_halo, pair_spill)

    places = shots * strips

    def gram_kernel(own, pair, other, out, pieces_out):
        _, even = where_am_i()
        top = own[:, :rim] + jnp.where(even, other[...], pair[...])
        bottom = own[:, cells - rim :] + jnp.where(even, pair[...], other[...])
        middle = own[:, rim : cells - rim]
        out[:, :rim] = top
        out[:, rim : cells - rim] = middle
        out[:, cells - rim :] = bottom
        total = jnp.zeros((3 * rank, 3 * rank), jnp.float32)
        for piece in (top, middle, bottom):
            stack = jnp.concatenate(parts_of(piece, 3), 0)
            total = total + dot32(stack, stack, NT)
        wide = total[:, :rank] + total[:, rank : 2 * rank] + total[:, 2 * rank :]
        gram = wide[:rank] + wide[rank : 2 * rank] + wide[2 * rank :]
        gram = jnp.concatenate(
            [gram[:half], gram[half:], jnp.zeros((half, LANES - 2 * rank), jnp.float32)], 1
        )
        for place in range(places):
            pieces_out[place] = gram

    sketch, gram_pieces = call(
        gram_kernel, [f32(rank, cells), f32(places, rank // 2, LANES)], 12, name="gram"
    )(sketch_own, pair_add, other_add)
    sketch_other = lax.ppermute(sketch, "shot", to_other)
    gram_pieces = lax.all_to_all(gram_pieces, ("shot", "strip"), 0, 0)

    def factor_kernel(grams, own, theirs, left_out, right_out, held, sems):
        side, _ = where_am_i()
        line = lax.broadcasted_iota(jnp.int32, (rank, rank), 0)
        column = lax.broadcasted_iota(jnp.int32, (rank, rank), 1)
        tall_line = lax.broadcasted_iota(jnp.int32, (rank, LANES), 0)
        sides = []
        for shot in range(2):
            halves = jnp.sum(grams[shot * strips : (shot + 1) * strips], 0)
            gram = jnp.concatenate([halves[:, :rank], halves[:, rank : 2 * rank]], 0)
            columns = [jnp.broadcast_to(gram[:, j : j + 1], (rank, LANES)) for j in range(rank)]
            sides.append((columns, [jnp.where(line == column, 1.0, 0.0)]))
        for j in range(rank):
            for columns, inverse in sides:
                factor = columns[j] * (1.0 / columns[j][j : j + 1])
                factor = jnp.where(tall_line > j, factor, 0.0)
                for k in range(j + 1, rank):
                    columns[k] = columns[k] - factor * columns[k][j : j + 1]
                inverse[0] = inverse[0] - factor[:, :rank] * inverse[0][j : j + 1]
        copies = []
        for (columns, inverse), shot, out in zip(sides, (0, 1), (left_out, right_out)):
            pivots = columns[0]
            for j in range(1, rank):
                pivots = jnp.where(tall_line == j, columns[j], pivots)
            inverse = inverse[0] * (lax.rsqrt(pivots[:, :rank]) * factor_scale)
            stack = jnp.concatenate(parts_of(inverse, 3), 0)
            stack = jnp.concatenate([stack] * 3, 1)
            for block in range(0, rows, 8):
                span = slice(block * cols, (block + 8) * cols)
                lines = jnp.where(side == shot, own[:, span], theirs[:, span])
                thick = jnp.concatenate(parts_of(lines, 3), 0)
                solved = jnp.dot(stack, thick, preferred_element_type=jnp.float32)
                solved = solved[:rank] + solved[rank : 2 * rank] + solved[2 * rank :]
                for t in range(0, cols, LANES):
                    tile = [solved[:, r * cols + t : r * cols + t + LANES][None] for r in range(8)]
                    held[shot, :, block : block + 8, t : t + LANES] = jnp.swapaxes(
                        jnp.concatenate(tile, 0), 0, 1
                    )
                lines_here = pl.ds(block, 8)
                copies.append(
                    pltpu.make_async_copy(
                        held.at[shot, :, lines_here], out.at[:, lines_here], sems.at[shot, block // 8]
                    )
                )
                copies[-1].start()
        for copy in copies:
            copy.wait()

    factor = f32(rank, rows, cols)
    left_factor, right_factor = pl.pallas_call(
        factor_kernel,
        out_shape=[factor, factor],
        in_specs=[near] * 3,
        out_specs=[far] * 2,
        scratch_shapes=[
            pltpu.VMEM((2, rank, rows, cols), jnp.float32),
            pltpu.SemaphoreType.DMA((2, rows // 8)),
        ],
        compiler_params=pltpu.CompilerParams(vmem_limit_bytes=12 * MIB),
        name="factors",
    )(gram_pieces, sketch, sketch_other)
    return left_factor, right_factor


def solution(mesh):
    return jax.shard_map(
        shards,
        mesh=mesh,
        in_specs=(
            P("shot", None, "strip", None),
            P("shot", None, "strip", None),
            P("shot", None, "strip", None),
            P("shot", None, "strip", None),
            P("strip", None),
            P(None, "strip", None),
            P(None, "strip", None),
        ),
        out_specs=(P(None, "strip", None), P(None, "strip", None)),
        check_vma=False,
    )
```

time: 63.7 us -> 58.8 us (0.923)
  waiting for transfers between devices: 9.32 us -> 0.15 us
  local copies, waits for them, and re-layouts: 0.01 us -> 2.41 us
  blocking collectives: 27.2 us -> 29.2 us
  starting transfers between devices: 8.4 us -> 6.87 us
  Pallas kernels: 17.9 us -> 19 us
    ppermute x1, waiting for transfers between devices: 4.19 us -> 0.01 us  [shards(): pair_add = lax.ppermute(pair_spill, 'strip', to_pair)]
    ppermute x1, starting transfers between devices: 5.73 us -> 2.57 us  [shards(): pair_halo = lax.ppermute(pair_edge, 'strip', to_pair)]
    ppermute x2 -> x4, waiting for transfers between devices: 3.09 us -> 0.13 us  [the longest x1 0.13 us: shards(): inner_other = lax.ppermute(inner_own, 'shot', to_other)]
    unnamed x2 -> x10, local copies, waits for them, and re-layouts: 0.01 us -> 2.41 us
    pallas_call x7 -> x10, Pallas kernels: 12.1 us -> 14.3 us  [the longest x1 2.55 us: shards(): call(product_kernel, [f32(rank, waves)] * 2 + [jax.ShapeDtypeStruct((2, 2...]
    ppermute x1, waiting for transfers between devices: 2.03 us -> 0.01 us  [shards(): pair_halo = lax.ppermute(pair_edge, 'strip', to_pair)]
    all_to_all x1, blocking collectives: 13.5 us -> 15.5 us  [shards(): pieces = lax.all_to_all(pieces, ('shot', 'strip'), 0, 0)]
    ppermute x2 -> x4, starting transfers between devices: 0.11 us -> 1.39 us  [the longest x1 0.51 us: shards(): rim_raw = lax.ppermute(rim_stage, 'shot', to_other)]
  transfers between devices with their start and end apart: 7 -> 9, of which waited for: 4 -> 1; matrix products, arithmetic and copies ran while one was open for 0% -> 0% of each run, Pallas kernels for 10% -> 24%
where the time goes in v1:
time: 58.8 us; the launch traced here: 58.6 us
  blocking collectives  29.2 us (50%)
  Pallas kernels  19 us (32%)
  starting transfers between devices  6.87 us (12%)
  local copies, waits for them, and re-layouts  2.41 us (4%)
  between operations  0.97 us (2%)
    all_to_all x1, blocking collectives, shards(): pieces = lax.all_to_all(pieces, ('shot', 'strip'), 0, 0)  15.5 us
    all_to_all x1, blocking collectives, shards(): gram_pieces = lax.all_to_all(gram_pieces, ('shot', 'strip'), 0, 0)  13.8 us
    pallas_call x1, Pallas kernels, shards(): pl.pallas_call(split_kernel, out_shape=[jax.ShapeDtypeStruct((2, 2, 2 * w...  2.97 us
    ppermute x1, starting transfers between devices, shards(): pair_halo = lax.ppermute(pair_edge, 'strip', to_pair)  2.57 us
    pallas_call x1, Pallas kernels, shards(): call(product_kernel, [f32(rank, waves)] * 2 + [jax.ShapeDtypeStruct((2, 2...  2.55 us
    pallas_call x1, Pallas kernels, shards(): call(sketch_kernel, f32(rank, cells), 16, [lines, lines, pltpu.VMEM((tall...  2.51 us
    unnamed x10, local copies, waits for them, and re-layouts  2.41 us
    pallas_call x1, Pallas kernels, shards(): pl.pallas_call(factor_kernel, out_shape=[factor, factor], in_specs=[near]...  1.88 us
  transfers between devices with their start and end apart: 9, of which 1 were waited for; matrix products, arithmetic and copies ran while one was open for 0% of the time, Pallas kernels for 24%

profile of v1, /device:TPU:0, one launch (start us, length us, event | category | flops | bytes accessed | tf_op | source)
XLA Modules:
  0.0 58.6 jit_solution(13564376233601273959)
XLA Ops:
  0.7 1.2 %edges.1 = (f32[17,8,256]{2,1,0:T(8,128)S(1)}, f32[17,8,256]{2,1,0:T(8,128)S(1)}) custom-call(f32[16,32,256]{2,1,0:T(8,128)} %left.3, f32[16,32,256]{2,1,0:T(8,128)} %right.3, f32[32,256]{1,0:T(8,128)} %speed.9), custom_call_target="tpu_custom_call" | custom-call | flops 20000000000 | bytes 4194304 | tf_op jit(solution)/shard_map/edges/pallas_call | solution.py:132
  1.9 0.5 copy-done
  2.4 0.6 %copy-done.1 = f32[1,64,32,256]{3,2,1,0:T(8,128)S(1)} copy-done((f32[1,64,32,256]{3,2,1,0:T(8,128)S(1)}, f32[1,64,32,256]{3,2,1,0:T(8,128)}, u32[]{:S(2)}) %copy-start.1) | copy-done | bytes 2097176
  3.0 0.6 %copy-done.2 = f32[1,64,32,256]{3,2,1,0:T(8,128)S(1)} copy-done((f32[1,64,32,256]{3,2,1,0:T(8,128)S(1)}, f32[1,64,32,256]{3,2,1,0:T(8,128)}, u32[]{:S(2)}) %copy-start.2) | copy-done | bytes 2097176
  3.7 0.6 %copy-done.3 = f32[1,64,32,256]{3,2,1,0:T(8,128)S(1)} copy-done((f32[1,64,32,256]{3,2,1,0:T(8,128)S(1)}, f32[1,64,32,256]{3,2,1,0:T(8,128)}, u32[]{:S(2)}) %copy-start.3) | copy-done | bytes 2097176
  4.3 0.2 stage.1
  4.5 0.5 collective-permute-start.4
  5.0 2.6 %collective-permute-start = (f32[17,8,256]{2,1,0:T(8,128)S(1)}, f32[17,8,256]{2,1,0:T(8,128)S(1)}, u32[]{:S(2)}, u32[]{:S(2)}) collective-permute-start(f32[17,8,256]{2,1,0:T(8,128)S(1)} %get-tuple-element.18._), channel_id=1, source_target_pairs={{0,1},{1,0},{2,3},{3,2},{4,5},{5,4},{6,7},{7,6},{8,9},{9,8},{10,11... | collective-permute-start | bytes 417800 | tf_op jit(solution)/shard_map/ppermute | solution.py:143
  7.5 0.8 %collective-permute-start.1 = (f32[17,8,256]{2,1,0:T(8,128)S(1)}, f32[17,8,256]{2,1,0:T(8,128)S(1)}, u32[]{:S(2)}, u32[]{:S(2)}) collective-permute-start(f32[17,8,256]{2,1,0:T(8,128)S(1)} %get-tuple-element.23), channel_id=1, source_target_pairs={{1,2},{3,4},{5,6},{7,8},{9,10},{11,12},{13,14},{2,1},{4,3},{6,5},{... | collective-permute-start | bytes 417800 | tf_op jit(solution)/shard_map/ppermute | solution.py:142
  8.3 3.0 %split.1 = (bf16[2,2,128,8192]{3,2,1,0:T(8,128)(2,1)S(1)}, f32[32,16,256]{2,1,0:T(8,128)S(1)}, f32[2,64,16,256]{3,2,1,0:T(8,128)S(1)}) custom-call(f32[64,32,256]{2,1,0:T(8,128)S(1)} %bitcast.5, f32[64,32,256]{2,1,0:T(8,128)S(1)} %bitcast.7, f32[64,32,256]{2,1,0:T(8,128)S(1)} %bitcast.9, f32[64,32,256]{2,1,0:T(8,128)S(1)} %bitcast.11, f32[16,32,256]{2,1,0:T(8,128)} %left.3, ...), custom_call_target="tpu_custom_call" | custom-call | bytes 16777216 | tf_op jit(solution)/shard_map/split/pallas_call | solution.py:218
  11.3 1.7 %probes_inner.1 = (f32[2,16,4096]{2,1,0:T(8,128)S(1)}, f32[8,4,16,256]{3,2,1,0:T(8,128)S(1)}) custom-call(f32[32,16,256]{2,1,0:T(8,128)S(1)} %get-tuple-element.21.begin, f32[32,256]{1,0:T(8,128)S(1)} %copy-done.4), custom_call_target="tpu_custom_call" | custom-call | tf_op jit(solution)/shard_map/probes_inner/pallas_call | solution.py:260
  13.0 0.2 collective-permute-start.3
  13.2 0.0 collective-permute-done.pair
  13.2 0.0 collective-permute-done.1.other
  13.2 1.2 %probes_rim.1.rim_mine = f32[2,16,4096]{2,1,0:T(8,128)S(1)} custom-call(f32[8,4,16,256]{3,2,1,0:T(8,128)S(1)} %get-tuple-element.22.saved, f32[32,256]{1,0:T(8,128)S(1)} %copy-done.4, f32[17,8,256]{2,1,0:T(8,128)S(1)} %collective-permute-done.pair, f32[17,8,256]{2,1,0:T(8,128)S(1)} %collective-permute-done.1.other), custom_call_target="tpu_custom_call" | custom-call | tf_op jit(solution)/shard_map/probes_rim/pallas_call | solution.py:306
  14.4 0.4 collective-permute-start.2
  14.9 0.1 collective-permute-done.3.inner_theirs
  15.0 0.0 collective-permute-done.4.raw
  15.0 2.5 %product.1 = (f32[16,64]{1,0:T(8,128)S(1)}, f32[16,64]{1,0:T(8,128)S(1)}, bf16[2,128,4096]{2,1,0:T(8,128)(2,1)S(1)}) custom-call(bf16[2,2,128,8192]{3,2,1,0:T(8,128)(2,1)S(1)} %get-tuple-element.20.fields_ref, f32[2,16,4096]{2,1,0:T(8,128)S(1)} %get-tuple-element.24.inner_mine, f32[2,16,4096]{2,1,0:T(8,128)S(1)} %collective-permute-done.3.inner_theirs, ...), custom_call_target="tpu_custom_call" | custom-call | tf_op jit(solution)/shard_map/product/pallas_call | solution.py:356
  17.5 0.9 %product_last.1 = f32[32,8,128]{2,1,0:T(8,128)S(1)} custom-call(bf16[2,2,128,8192]{3,2,1,0:T(8,128)(2,1)S(1)} %get-tuple-element.20.fields_ref, f32[2,16,4096]{2,1,0:T(8,128)S(1)} %collective-permute-done.2.rim_theirs, f32[16,64]{1,0:T(8,128)S(1)} %get-tuple-element.25.mine_ref, f32[16,64]{1,0:T(8,128)S(1)} %get-tuple-element.26.theirs_ref), custom_call_target="tpu_custom_call" | custom-call | tf_op jit(solution)/shard_map/product_last/pallas_call | solution.py:362
  18.4 0.2 collective-permute-start.5
  18.7 15.5 %all_to_all.10.pieces_ref = f32[32,8,128]{2,1,0:T(8,128)S(1)} all-to-all(f32[32,8,128]{2,1,0:T(8,128)S(1)} %product_last.1), channel_id=1, replica_groups=mesh['shot'=2,'strip'=16] {'shot','strip'}, dimensions={0} | all-to-all | bytes 262144 | tf_op jit(solution)/shard_map/all_to_all | solution.py:367
  34.1 0.8 %terms_rim.1.own.rim_part = f32[2,16,4096]{2,1,0:T(8,128)S(1)} custom-call(f32[32,8,128]{2,1,0:T(8,128)S(1)} %all_to_all.10.pieces_ref, bf16[2,2,128,8192]{3,2,1,0:T(8,128)(2,1)S(1)} %get-tuple-element.20.fields_ref, bf16[2,128,4096]{2,1,0:T(8,128)(2,1)S(1)} %get-tuple-element.28.swapped_ref), custom_call_target="tpu_custom_call" | custom-call | flops 134217728 | tf_op jit(solution)/shard_map/terms_rim/pallas_call | solution.py:400
  35.0 1.1 %spill.1 = (f32[16,2048]{1,0:T(8,128)S(1)}, f32[16,2048]{1,0:T(8,128)S(1)}) custom-call(f32[2,16,4096]{2,1,0:T(8,128)S(1)} %terms_rim.1.own.rim_part, f32[32,256]{1,0:T(8,128)S(1)} %copy-done.4, f32[17,8,256]{2,1,0:T(8,128)S(1)} %collective-permute-done.pair, f32[17,8,256]{2,1,0:T(8,128)S(1)} %collective-permute-done.1.other), custom_call_target="tpu_custom_call" | custom-call | tf_op jit(solution)/shard_map/spill/pallas_call | solution.py:435
  36.1 1.2 %collective-permute-start.6 = (f32[16,2048]{1,0:T(8,128)S(1)}, f32[16,2048]{1,0:T(8,128)S(1)}, u32[]{:S(2)}, u32[]{:S(2)}) collective-permute-start(f32[16,2048]{1,0:T(8,128)S(1)} %get-tuple-element.30._), channel_id=1, source_target_pairs={{0,1},{1,0},{2,3},{3,2},{4,5},{5,4},{6,7},{7,6},{8,9},{9,8},{10,11... | collective-permute-start | bytes 393224 | tf_op jit(solution)/shard_map/ppermute | solution.py:443
  37.3 0.8 %collective-permute-start.7 = (f32[16,2048]{1,0:T(8,128)S(1)}, f32[16,2048]{1,0:T(8,128)S(1)}, u32[]{:S(2)}, u32[]{:S(2)}) collective-permute-start(f32[16,2048]{1,0:T(8,128)S(1)} %get-tuple-element.31), channel_id=1, source_target_pairs={{1,2},{3,4},{5,6},{7,8},{9,10},{11,12},{13,14},{2,1},{4,3},{6,5},{... | collective-permute-start | bytes 393224 | tf_op jit(solution)/shard_map/ppermute | solution.py:442
  38.2 1.5 %terms_inner.1.inner_part = f32[2,16,4096]{2,1,0:T(8,128)S(1)} custom-call(f32[32,8,128]{2,1,0:T(8,128)S(1)} %all_to_all.10.pieces_ref, bf16[2,2,128,8192]{3,2,1,0:T(8,128)(2,1)S(1)} %get-tuple-element.20.fields_ref, f32[2,64,16,256]{3,2,1,0:T(8,128)S(1)} %collective-permute-done.5.raw, f32[16,2048]{1,0:T(8,128)S(1)} %get-tuple-element.30._), custom_call_target="tpu_custom_call" | custom-call | flops 134217728 | tf_op jit(solution)/shard_map/terms_inner/pallas_call | solution.py:445
  39.7 2.5 %sketch.1.own = f32[16,8192]{1,0:T(8,128)S(1)} custom-call(f32[2,16,4096]{2,1,0:T(8,128)S(1)} %terms_rim.1.own.rim_part, f32[2,16,4096]{2,1,0:T(8,128)S(1)} %terms_inner.1.inner_part, f32[32,256]{1,0:T(8,128)S(1)} %copy-done.4, f32[17,8,256]{2,1,0:T(8,128)S(1)} %collective-permute-done.pair, f32[17,8,256]{2,1,0:T(8,128)S(1)} %collective-permute-done.1.other, ...), custom_call_target="tpu_custom_call" | custom-call | bytes 8388608 | tf_op jit(solution)/shard_map/sketch/pallas_call | solution.py:485
  42.2 0.5 gram.1
  42.7 0.1 collective-permute-start.8
  42.8 13.8 %all_to_all.11.grams = f32[32,8,128]{2,1,0:T(8,128)S(1)} all-to-all(f32[32,8,128]{2,1,0:T(8,128)S(1)} %get-tuple-element.32), channel_id=1, replica_groups=mesh['shot'=2,'strip'=16] {'shot','strip'}, dimensions={0} | all-to-all | bytes 262144 | tf_op jit(solution)/shard_map/all_to_all | solution.py:520
  56.6 1.9 %factors.1 = (f32[16,32,256]{2,1,0:T(8,128)}, f32[16,32,256]{2,1,0:T(8,128)}) custom-call(f32[32,8,128]{2,1,0:T(8,128)S(1)} %all_to_all.11.grams, f32[16,8192]{1,0:T(8,128)S(1)} %get-tuple-element.33.own, f32[16,8192]{1,0:T(8,128)S(1)} %collective-permute-done.8.theirs), custom_call_target="tpu_custom_call" | custom-call | tf_op jit(solution)/shard_map/factors/pallas_call | solution.py:570
  (11 shorter events, 0.0 us)
Async XLA Ops:
  0.6 1.8 %copy-start = (f32[1,64,32,256]{3,2,1,0:T(8,128)S(1)}, f32[1,64,32,256]{3,2,1,0:T(8,128)}, u32[]{:S(2)}) copy-start(f32[1,64,32,256]{3,2,1,0:T(8,128)} %param.9) | copy-start | bytes 6291460
  0.6 2.4 %copy-start.1 = (f32[1,64,32,256]{3,2,1,0:T(8,128)S(1)}, f32[1,64,32,256]{3,2,1,0:T(8,128)}, u32[]{:S(2)}) copy-start(f32[1,64,32,256]{3,2,1,0:T(8,128)} %param.10) | copy-start | bytes 6291460
  0.7 3.0 %copy-start.2 = (f32[1,64,32,256]{3,2,1,0:T(8,128)S(1)}, f32[1,64,32,256]{3,2,1,0:T(8,128)}, u32[]{:S(2)}) copy-start(f32[1,64,32,256]{3,2,1,0:T(8,128)} %param.7) | copy-start | bytes 6291460
  0.7 3.6 %copy-start.3 = (f32[1,64,32,256]{3,2,1,0:T(8,128)S(1)}, f32[1,64,32,256]{3,2,1,0:T(8,128)}, u32[]{:S(2)}) copy-start(f32[1,64,32,256]{3,2,1,0:T(8,128)} %param.8) | copy-start | bytes 6291460
  4.5 10.5 %collective-permute-start.4 = (f32[2,64,16,256]{3,2,1,0:T(8,128)S(1)}, f32[2,64,16,256]{3,2,1,0:T(8,128)S(1)}, u32[]{:S(2)}, u32[]{:S(2)}) collective-permute-start(f32[2,64,16,256]{3,2,1,0:T(8,128)S(1)} %stage.1), channel_id=1, source_target_pairs={{0,16},{16,0},{1,17},{17,1},{2,18},{18,2},{3,19},{19,3},{4,20},{20... | collective-permute-start | bytes 6291464 | tf_op jit(solution)/shard_map/ppermute | solution.py:240
  5.0 8.3 %collective-permute-start = (f32[17,8,256]{2,1,0:T(8,128)S(1)}, f32[17,8,256]{2,1,0:T(8,128)S(1)}, u32[]{:S(2)}, u32[]{:S(2)}) collective-permute-start(f32[17,8,256]{2,1,0:T(8,128)S(1)} %get-tuple-element.18._), channel_id=1, source_target_pairs={{0,1},{1,0},{2,3},{3,2},{4,5},{5,4},{6,7},{7,6},{8,9},{9,8},{10,11... | collective-permute-start | bytes 417800 | tf_op jit(solution)/shard_map/ppermute | solution.py:143
  7.5 3.8 %copy-start.4 = (f32[32,256]{1,0:T(8,128)S(1)}, f32[32,256]{1,0:T(8,128)}, u32[]{:S(2)}) copy-start(f32[32,256]{1,0:T(8,128)} %speed.9) | copy-start | bytes 98308
  7.5 5.7 %collective-permute-start.1 = (f32[17,8,256]{2,1,0:T(8,128)S(1)}, f32[17,8,256]{2,1,0:T(8,128)S(1)}, u32[]{:S(2)}, u32[]{:S(2)}) collective-permute-start(f32[17,8,256]{2,1,0:T(8,128)S(1)} %get-tuple-element.23), channel_id=1, source_target_pairs={{1,2},{3,4},{5,6},{7,8},{9,10},{11,12},{13,14},{2,1},{4,3},{6,5},{... | collective-permute-start | bytes 417800 | tf_op jit(solution)/shard_map/ppermute | solution.py:142
  13.0 2.0 %collective-permute-start.3 = (f32[2,16,4096]{2,1,0:T(8,128)S(1)}, f32[2,16,4096]{2,1,0:T(8,128)S(1)}, u32[]{:S(2)}, u32[]{:S(2)}) collective-permute-start(f32[2,16,4096]{2,1,0:T(8,128)S(1)} %get-tuple-element.24.inner_mine), channel_id=1, source_target_pairs={{0,16},{16,0},{1,17},{17,1},{2,18},{18,2},{3,19},{19,3},{4,20},{20... | collective-permute-start | bytes 1572872 | tf_op jit(solution)/shard_map/ppermute | solution.py:267
  14.4 3.1 %collective-permute-start.2 = (f32[2,16,4096]{2,1,0:T(8,128)S(1)}, f32[2,16,4096]{2,1,0:T(8,128)S(1)}, u32[]{:S(2)}, u32[]{:S(2)}) collective-permute-start(f32[2,16,4096]{2,1,0:T(8,128)S(1)} %probes_rim.1.rim_mine), channel_id=1, source_target_pairs={{0,16},{16,0},{1,17},{17,1},{2,18},{18,2},{3,19},{19,3},{4,20},{20... | collective-permute-start | bytes 1572872 | tf_op jit(solution)/shard_map/ppermute | solution.py:313
  18.4 19.7 %collective-permute-start.5 = (f32[2,64,16,256]{3,2,1,0:T(8,128)S(1)}, f32[2,64,16,256]{3,2,1,0:T(8,128)S(1)}, u32[]{:S(2)}, u32[]{:S(2)}) collective-permute-start(f32[2,64,16,256]{3,2,1,0:T(8,128)S(1)} %get-tuple-element.29), channel_id=1, source_target_pairs={{0,16},{16,0},{1,17},{17,1},{2,18},{18,2},{3,19},{19,3},{4,20},{20... | collective-permute-start | bytes 6291464 | tf_op jit(solution)/shard_map/ppermute | solution.py:366
  36.1 6.1 %collective-permute-start.6 = (f32[16,2048]{1,0:T(8,128)S(1)}, f32[16,2048]{1,0:T(8,128)S(1)}, u32[]{:S(2)}, u32[]{:S(2)}) collective-permute-start(f32[16,2048]{1,0:T(8,128)S(1)} %get-tuple-element.30._), channel_id=1, source_target_pairs={{0,1},{1,0},{2,3},{3,2},{4,5},{5,4},{6,7},{7,6},{8,9},{9,8},{10,11... | collective-permute-start | bytes 393224 | tf_op jit(solution)/shard_map/ppermute | solution.py:443
  37.3 4.9 %collective-permute-start.7 = (f32[16,2048]{1,0:T(8,128)S(1)}, f32[16,2048]{1,0:T(8,128)S(1)}, u32[]{:S(2)}, u32[]{:S(2)}) collective-permute-start(f32[16,2048]{1,0:T(8,128)S(1)} %get-tuple-element.31), channel_id=1, source_target_pairs={{1,2},{3,4},{5,6},{7,8},{9,10},{11,12},{13,14},{2,1},{4,3},{6,5},{... | collective-permute-start | bytes 393224 | tf_op jit(solution)/shard_map/ppermute | solution.py:442
  42.7 13.8 %collective-permute-start.8 = (f32[16,8192]{1,0:T(8,128)S(1)}, f32[16,8192]{1,0:T(8,128)S(1)}, u32[]{:S(2)}, u32[]{:S(2)}) collective-permute-start(f32[16,8192]{1,0:T(8,128)S(1)} %get-tuple-element.33.own), channel_id=1, source_target_pairs={{0,16},{16,0},{1,17},{17,1},{2,18},{18,2},{3,19},{19,3},{4,20},{20... | collective-permute-start | bytes 1572872 | tf_op jit(solution)/shard_map/ppermute | solution.py:519

commit v2 on v1

--- a/solution.py
+++ b/solution.py
@@ -103,6 +103,10 @@
             made = []
             for index, (out, start) in enumerate(((pair, pair_row), (other, other_row))):
                 start = pl.multiple_of(start, 8)
+                if out.shape[0] > rank + 1:
+                    made.append(
+                        pltpu.make_async_copy(speed.at[pl.ds(start, edge), :], out.at[rank + 1], sem.at[4])
+                    )
                 made.append(
                     pltpu.make_async_copy(
                         probe.at[:, pl.ds(start, edge), :], out.at[pl.ds(0, rank)], sem.at[2 * index]
@@ -131,10 +135,10 @@
     near = pl.BlockSpec(memory_space=pltpu.VMEM)
     pair_edge, other_edge = pl.pallas_call(
         edges_kernel,
-        out_shape=[halo, halo],
+        out_shape=[f32(rank + 2, edge, cols), halo],
         in_specs=[far] * 3,
         out_specs=[near] * 2,
-        scratch_shapes=[pltpu.SemaphoreType.DMA((4,))],
+        scratch_shapes=[pltpu.SemaphoreType.DMA((5,))],
         compiler_params=pltpu.CompilerParams(vmem_limit_bytes=4 * MIB),
         cost_estimate=pl.CostEstimate(flops=20000000000, bytes_accessed=4194304, transcendentals=0),
         name="edges",
@@ -153,7 +157,7 @@
 
     def split_kernel(
         adjoint_a, adjoint_b, source_a, source_b, left, right, speeds, _,
-        out, start, inner_stage, probe, speed, sem,
+        out, start, stage, probe, speed, sem,
     ):
         side, _ = where_am_i()
 
@@ -179,9 +183,7 @@
                     for t in range(0, cols, LANES):
                         span = slice(t, t + LANES)
                         mine, other = adjoint[some, block : block + 8, span], source[some, block : block + 8, span]
-                        if edge <= block < rows - edge:
-                            sent = jnp.where(side == 0, mine, other)
-                            inner_stage[level, some, block - edge : block - edge + 8, span] = sent
+                        stage[level, some, block : block + 8, span] = jnp.where(side == 0, mine, other)
                         lay_out(mine, out.at[0, level], some, low, block, t)
                         lay_out(other, out.at[1, level], some, low, block, t)
         speed_copy.wait()
@@ -190,37 +192,12 @@
             span = slice(block, block + 8)
             start[span] = rows_first(probe[:, span, :]) * speed[span, :][:, None, :]
 
-    def stage_kernel(adjoint_a, adjoint_b, source_a, source_b, _, out):
-        side, _ = where_am_i()
-
-        def stage(pair):
-            for level, ref in enumerate(pair):
-                out[level, :, :edge] = ref[:, :edge]
-                out[level, :, edge:] = ref[:, rows - edge :]
-
-        @pl.when(side == 0)
-        def _():
-            stage((adjoint_a, adjoint_b))
-
-        @pl.when(side != 0)
-        def _():
-            stage((source_a, source_b))
-
-    kinds = (adjoint_now[0], adjoint_prev[0], source_now[0], source_prev[0])
-    rim_stage = pl.pallas_call(
-        stage_kernel,
-        out_shape=f32(2, waves, 2 * edge, cols),
-        in_specs=[near] * 4 + [pl.BlockSpec(memory_space=pl.ANY)],
-        out_specs=near,
-        compiler_params=pltpu.CompilerParams(vmem_limit_bytes=26 * MIB),
-        name="stage",
-    )(*kinds, pair_edge)
-    fields, start, inner_stage = pl.pallas_call(
+    fields, start, stage = pl.pallas_call(
         split_kernel,
         out_shape=[
             jax.ShapeDtypeStruct((2, 2, 2 * waves, cells), jnp.bfloat16),
             f32(rows, rank, cols),
-            f32(2, waves, rows - 2 * edge, cols),
+            f32(2, waves, rows, cols),
         ],
         in_specs=[near] * 4 + [far] * 3 + [pl.BlockSpec(memory_space=pl.ANY)],
         out_specs=[near] * 3,
@@ -233,12 +210,10 @@
         cost_estimate=pl.CostEstimate(flops=0, bytes_accessed=16 * waves * cells * 2, transcendentals=0),
         name="split",
     )(
-        *kinds,
+        adjoint_now[0], adjoint_prev[0], source_now[0], source_prev[0],
         *map(in_hbm, (probe_left, probe_right, courant)),
         pair_edge,
     )
-    rim_raw = lax.ppermute(rim_stage, "shot", to_other)
-
     inner = rows - 2 * edge
     rim = edge * cols
 
@@ -322,23 +297,22 @@
         total = total[:waves] + total[waves:]
         return (total[:, :rank] + total[:, rank:]).T
 
-    def product_kernel(fields_ref, inner_mine, inner_theirs, rim_mine, raw, mine, theirs, swapped):
+    def product_kernel(fields_ref, inner_mine, inner_theirs, rim_mine, mine, theirs):
         side, _ = where_am_i()
         mine[...] = products(fields_ref, inner_mine, side, True) + products(
             fields_ref, rim_mine, side, False
         )
         theirs[...] = products(fields_ref, inner_theirs, 1 - side, True)
-        lay_out_raw(raw, swapped)
-
-    def lay_out_raw(raw, out):
+
+    def lay_out_raw(raw, blocks, out):
         for level in range(2):
             for first in range(0, waves, group):
                 some = slice(first, first + group)
                 low = slice(waves + first, waves + first + group)
-                for block in range(0, raw.shape[2], 8):
+                for place, block in enumerate(blocks):
                     for t in range(0, cols, LANES):
                         piece = raw[level, some, block : block + 8, t : t + LANES]
-                        lay_out(piece, out.at[level], some, low, block, t)
+                        lay_out(piece, out.at[level], some, low, 8 * place, t)
 
     half = rank // 2
 
@@ -353,17 +327,14 @@
                 out[shot * strips + strip] = weights
 
     flops = 2 * 2 * waves * 2 * rank * cells * 2
-    mine, theirs, rim_swapped = call(
-        product_kernel,
-        [f32(rank, waves)] * 2 + [jax.ShapeDtypeStruct((2, 2 * waves, 2 * rim), jnp.bfloat16)],
-        24,
-        name="product",
-    )(fields, inner_own, inner_other, rim_own, rim_raw)
+    mine, theirs = call(product_kernel, [f32(rank, waves)] * 2, 24, name="product")(
+        fields, inner_own, inner_other, rim_own
+    )
     pieces = call(
         product_last_kernel, f32(shots * strips, half, 2 * waves), 24, name="product_last"
     )(fields, rim_other, mine, theirs)
-    inner_stage, pieces = lax.optimization_barrier((inner_stage, pieces))
-    inner_raw = lax.ppermute(inner_stage, "shot", to_other)
+    stage, pieces = lax.optimization_barrier((stage, pieces))
+    raw = lax.ppermute(stage, "shot", to_other)
     pieces = lax.all_to_all(pieces, ("shot", "strip"), 0, 0)
 
     def combine(pieces_ref, fields_ref, swapped_ref, places, out):
@@ -389,17 +360,23 @@
                 )
                 out[level, :, place : place + count] = both[:rank] + both[rank:]
 
-    def rim_terms_kernel(pieces_ref, fields_ref, swapped_ref, out):
+    def rim_terms_kernel(pieces_ref, fields_ref, raw, out, swapped):
+        lay_out_raw(raw, [*range(0, edge, 8), *range(rows - edge, rows, 8)], swapped)
         places = [(0, 0, rim), (cells - rim, rim, rim)]
-        combine(pieces_ref, fields_ref, swapped_ref, places, out)
+        combine(pieces_ref, fields_ref, swapped, places, out)
 
     def inner_terms_kernel(pieces_ref, fields_ref, raw, _, out, swapped):
-        lay_out_raw(raw, swapped)
+        lay_out_raw(raw, range(edge, rows - edge, 8), swapped)
         combine(pieces_ref, fields_ref, swapped, [(rim, 0, inner * cols)], out)
 
     rim_terms = call(
-        rim_terms_kernel, f32(2, rank, 2 * rim), 24, name="terms_rim", flops=flops
-    )(pieces, fields, rim_swapped)
+        rim_terms_kernel,
+        f32(2, rank, 2 * rim),
+        24,
+        [pltpu.VMEM((2, 2 * waves, 2 * rim), jnp.bfloat16)],
+        name="terms_rim",
+        flops=flops,
+    )(pieces, fields, raw)
 
     def spill_kernel(
         own, speed, pair, other, pair_out, other_out,
@@ -425,6 +402,7 @@
             advance_rows(edge + 1 - step, 2 * edge + 1 - step, a, b, up_speed, False)
             advance_rows(step, edge + step, c, d, low_speed, False)
             a, b, c, d = b, a, d, c
+        pair_out[:, rim:] = jnp.zeros((rank, LANES), jnp.float32)
         for r in range(edge):
             span = slice(r * cols, (r + 1) * cols)
             upper, lower = a[1 + r], c[edge + r]
@@ -434,7 +412,7 @@
     spill = f32(rank, rim)
     pair_spill, other_spill = call(
         spill_kernel,
-        [spill, spill],
+        [f32(rank, rim + LANES), spill],
         16,
         [short] * 4 + [short_speed] * 2,
         name="spill",
@@ -449,7 +427,7 @@
         [pltpu.VMEM((2, 2 * waves, inner * cols), jnp.bfloat16)],
         name="terms_inner",
         flops=flops,
-    )(pieces, fields, inner_raw, pair_spill)
+    )(pieces, fields, raw, pair_spill)
     pad = STEPS // 2 + 1
     tall = rows + 2 * pad
 
@@ -495,8 +473,8 @@
 
     def gram_kernel(own, pair, other, out, pieces_out):
         _, even = where_am_i()
-        top = own[:, :rim] + jnp.where(even, other[...], pair[...])
-        bottom = own[:, cells - rim :] + jnp.where(even, pair[...], other[...])
+        top = own[:, :rim] + jnp.where(even, other[:, :rim], pair[:, :rim])
+        bottom = own[:, cells - rim :] + jnp.where(even, pair[:, :rim], other[:, :rim])
         middle = own[:, rim : cells - rim]
         out[:, :rim] = top
         out[:, rim : cells - rim] = middle

time: 58.8 us -> 56 us (0.952)
  local copies, waits for them, and re-layouts: 2.41 us -> 0.02 us
    unnamed x10, local copies, waits for them, and re-layouts: 2.41 us -> 0.02 us
    pallas_call x5 -> x4, Pallas kernels: 5.88 us -> 5.72 us  [the longest x1 1.89 us: shards(): call(product_kernel, [f32(rank, waves)] * 2, 24, name='product')]
  transfers between devices with their start and end apart: 9 -> 8, of which waited for: 1 -> 1; matrix products, arithmetic and copies ran while one was open for 0% -> 0% of each run, Pallas kernels for 24% -> 21%
where the time goes in v2:
time: 56 us; the launch traced here: 55.8 us
  blocking collectives  29.1 us (52%)
  Pallas kernels  19 us (34%)
  starting transfers between devices  6.6 us (12%)
  between operations  1 us (2%)
    all_to_all x1, blocking collectives, shards(): pieces = lax.all_to_all(pieces, ('shot', 'strip'), 0, 0)  15.3 us
    all_to_all x1, blocking collectives, shards(): gram_pieces = lax.all_to_all(gram_pieces, ('shot', 'strip'), 0, 0)  13.8 us
    pallas_call x1, Pallas kernels, shards(): pl.pallas_call(split_kernel, out_shape=[jax.ShapeDtypeStruct((2, 2, 2 * w...  3.01 us
    ppermute x1, starting transfers between devices, shards(): pair_halo = lax.ppermute(pair_edge, 'strip', to_pair)  3 us
    pallas_call x1, Pallas kernels, shards(): call(sketch_kernel, f32(rank, cells), 16, [lines, lines, pltpu.VMEM((tall...  2.52 us
    pallas_call x1, Pallas kernels, shards(): pl.pallas_call(factor_kernel, out_shape=[factor, factor], in_specs=[near]...  1.92 us
    pallas_call x1, Pallas kernels, shards(): call(product_kernel, [f32(rank, waves)] * 2, 24, name='product')  1.89 us
    pallas_call x1, Pallas kernels, shards(): call(inner_kernel, [f32(2, rank, inner * cols), f32(STEPS, 4, rank, cols)...  1.7 us
  transfers between devices with their start and end apart: 8, of which 1 were waited for; matrix products, arithmetic and copies ran while one was open for 0% of the time, Pallas kernels for 21%

profile of v2, /device:TPU:0, one launch (start us, length us, event | category | flops | bytes accessed | tf_op | source)
XLA Modules:
  0.0 55.8 jit_solution(9122472064297852978)
XLA Ops:
  0.7 1.2 %edges.1 = (f32[18,8,256]{2,1,0:T(8,128)S(1)}, f32[17,8,256]{2,1,0:T(8,128)S(1)}) custom-call(f32[16,32,256]{2,1,0:T(8,128)} %left.3, f32[16,32,256]{2,1,0:T(8,128)} %right.3, f32[32,256]{1,0:T(8,128)} %speed.9), custom_call_target="tpu_custom_call" | custom-call | flops 20000000000 | bytes 4194304 | tf_op jit(solution)/shard_map/edges/pallas_call | solution.py:136
  1.9 3.0 %collective-permute-start = (f32[18,8,256]{2,1,0:T(8,128)S(1)}, f32[18,8,256]{2,1,0:T(8,128)S(1)}, u32[]{:S(2)}, u32[]{:S(2)}) collective-permute-start(f32[18,8,256]{2,1,0:T(8,128)S(1)} %get-tuple-element.17._), channel_id=1, source_target_pairs={{0,1},{1,0},{2,3},{3,2},{4,5},{5,4},{6,7},{7,6},{8,9},{9,8},{10,11... | collective-permute-start | bytes 442376 | tf_op jit(solution)/shard_map/ppermute | solution.py:147
  4.9 0.7 %collective-permute-start.1 = (f32[17,8,256]{2,1,0:T(8,128)S(1)}, f32[17,8,256]{2,1,0:T(8,128)S(1)}, u32[]{:S(2)}, u32[]{:S(2)}) collective-permute-start(f32[17,8,256]{2,1,0:T(8,128)S(1)} %get-tuple-element.22), channel_id=1, source_target_pairs={{1,2},{3,4},{5,6},{7,8},{9,10},{11,12},{13,14},{2,1},{4,3},{6,5},{... | collective-permute-start | bytes 417800 | tf_op jit(solution)/shard_map/ppermute | solution.py:146
  5.6 0.0 copy-done.1
  5.6 0.0 copy-start.4
  5.6 3.0 %split.1 = (bf16[2,2,128,8192]{3,2,1,0:T(8,128)(2,1)S(1)}, f32[32,16,256]{2,1,0:T(8,128)S(1)}, f32[2,64,32,256]{3,2,1,0:T(8,128)S(1)}) custom-call(f32[64,32,256]{2,1,0:T(8,128)S(1)} %bitcast.4, f32[64,32,256]{2,1,0:T(8,128)S(1)} %bitcast.5, f32[64,32,256]{2,1,0:T(8,128)S(1)} %bitcast.6, f32[64,32,256]{2,1,0:T(8,128)S(1)} %bitcast.7, f32[16,32,256]{2,1,0:T(8,128)} %left.3, ...), custom_call_target="tpu_custom_call" | custom-call | bytes 16777216 | tf_op jit(solution)/shard_map/split/pallas_call | solution.py:195
  8.6 1.7 %probes_inner.1 = (f32[2,16,4096]{2,1,0:T(8,128)S(1)}, f32[8,4,16,256]{3,2,1,0:T(8,128)S(1)}) custom-call(f32[32,16,256]{2,1,0:T(8,128)S(1)} %get-tuple-element.20.begin, f32[32,256]{1,0:T(8,128)S(1)} %copy-done.4), custom_call_target="tpu_custom_call" | custom-call | tf_op jit(solution)/shard_map/probes_inner/pallas_call | solution.py:235
  10.3 0.1 collective-permute-start.3
  10.4 0.0 collective-permute-done.1.other
  10.4 0.0 collective-permute-done.pair
  10.4 1.2 %probes_rim.1.rim_mine = f32[2,16,4096]{2,1,0:T(8,128)S(1)} custom-call(f32[8,4,16,256]{3,2,1,0:T(8,128)S(1)} %get-tuple-element.21.saved, f32[32,256]{1,0:T(8,128)S(1)} %copy-done.4, f32[18,8,256]{2,1,0:T(8,128)S(1)} %collective-permute-done.pair, f32[17,8,256]{2,1,0:T(8,128)S(1)} %collective-permute-done.1.other), custom_call_target="tpu_custom_call" | custom-call | tf_op jit(solution)/shard_map/probes_rim/pallas_call | solution.py:281
  11.7 0.5 collective-permute-start.2
  12.2 0.1 collective-permute-done.3.inner_theirs
  12.3 1.9 %product.1 = (f32[16,64]{1,0:T(8,128)S(1)}, f32[16,64]{1,0:T(8,128)S(1)}) custom-call(bf16[2,2,128,8192]{3,2,1,0:T(8,128)(2,1)S(1)} %get-tuple-element.19.fields_ref, f32[2,16,4096]{2,1,0:T(8,128)S(1)} %get-tuple-element.23.inner_mine, f32[2,16,4096]{2,1,0:T(8,128)S(1)} %collective-permute-done.3.inner_theirs, f32[2,16,4096]{2,1,0:T(8,128)S(1)} %probes_rim.1.rim_mine), custom_call_target="tpu_custom_call" | custom-call | tf_op jit(solution)/shard_map/product/pallas_call | solution.py:330
  14.2 0.0 collective-permute-done.2.rim_theirs
  14.2 0.9 %product_last.1 = f32[32,8,128]{2,1,0:T(8,128)S(1)} custom-call(bf16[2,2,128,8192]{3,2,1,0:T(8,128)(2,1)S(1)} %get-tuple-element.19.fields_ref, f32[2,16,4096]{2,1,0:T(8,128)S(1)} %collective-permute-done.2.rim_theirs, f32[16,64]{1,0:T(8,128)S(1)} %get-tuple-element.24.mine_ref, f32[16,64]{1,0:T(8,128)S(1)} %get-tuple-element.25.theirs_ref), custom_call_target="tpu_custom_call" | custom-call | tf_op jit(solution)/shard_map/product_last/pallas_call | solution.py:333
  15.1 0.2 collective-permute-start.4
  15.3 15.3 %all_to_all.10.pieces_ref = f32[32,8,128]{2,1,0:T(8,128)S(1)} all-to-all(f32[32,8,128]{2,1,0:T(8,128)S(1)} %product_last.1), channel_id=1, replica_groups=mesh['shot'=2,'strip'=16] {'shot','strip'}, dimensions={0} | all-to-all | bytes 262144 | tf_op jit(solution)/shard_map/all_to_all | solution.py:338
  30.7 0.0 collective-permute-done.4.raw
  30.7 1.5 %terms_rim.1.own.rim_part = f32[2,16,4096]{2,1,0:T(8,128)S(1)} custom-call(f32[32,8,128]{2,1,0:T(8,128)S(1)} %all_to_all.10.pieces_ref, bf16[2,2,128,8192]{3,2,1,0:T(8,128)(2,1)S(1)} %get-tuple-element.19.fields_ref, f32[2,64,32,256]{3,2,1,0:T(8,128)S(1)} %collective-permute-done.4.raw), custom_call_target="tpu_custom_call" | custom-call | flops 134217728 | tf_op jit(solution)/shard_map/terms_rim/pallas_call | solution.py:372
  32.2 1.1 %spill.1 = (f32[16,2176]{1,0:T(8,128)S(1)}, f32[16,2048]{1,0:T(8,128)S(1)}) custom-call(f32[2,16,4096]{2,1,0:T(8,128)S(1)} %terms_rim.1.own.rim_part, f32[32,256]{1,0:T(8,128)S(1)} %copy-done.4, f32[18,8,256]{2,1,0:T(8,128)S(1)} %collective-permute-done.pair, f32[17,8,256]{2,1,0:T(8,128)S(1)} %collective-permute-done.1.other), custom_call_target="tpu_custom_call" | custom-call | tf_op jit(solution)/shard_map/spill/pallas_call | solution.py:413
  33.3 1.2 %collective-permute-start.5 = (f32[16,2176]{1,0:T(8,128)S(1)}, f32[16,2176]{1,0:T(8,128)S(1)}, u32[]{:S(2)}, u32[]{:S(2)}) collective-permute-start(f32[16,2176]{1,0:T(8,128)S(1)} %get-tuple-element.28._), channel_id=1, source_target_pairs={{0,1},{1,0},{2,3},{3,2},{4,5},{5,4},{6,7},{7,6},{8,9},{9,8},{10,11... | collective-permute-start | bytes 417800 | tf_op jit(solution)/shard_map/ppermute | solution.py:421
  34.5 0.8 %collective-permute-start.6 = (f32[16,2048]{1,0:T(8,128)S(1)}, f32[16,2048]{1,0:T(8,128)S(1)}, u32[]{:S(2)}, u32[]{:S(2)}) collective-permute-start(f32[16,2048]{1,0:T(8,128)S(1)} %get-tuple-element.29), channel_id=1, source_target_pairs={{1,2},{3,4},{5,6},{7,8},{9,10},{11,12},{13,14},{2,1},{4,3},{6,5},{... | collective-permute-start | bytes 393224 | tf_op jit(solution)/shard_map/ppermute | solution.py:420
  35.3 1.5 %terms_inner.1.inner_part = f32[2,16,4096]{2,1,0:T(8,128)S(1)} custom-call(f32[32,8,128]{2,1,0:T(8,128)S(1)} %all_to_all.10.pieces_ref, bf16[2,2,128,8192]{3,2,1,0:T(8,128)(2,1)S(1)} %get-tuple-element.19.fields_ref, f32[2,64,32,256]{3,2,1,0:T(8,128)S(1)} %collective-permute-done.4.raw, f32[16,2176]{1,0:T(8,128)S(1)} %get-tuple-element.28._), custom_call_target="tpu_custom_call" | custom-call | flops 134217728 | tf_op jit(solution)/shard_map/terms_inner/pallas_call | solution.py:423
  36.9 2.5 %sketch.1.own = f32[16,8192]{1,0:T(8,128)S(1)} custom-call(f32[2,16,4096]{2,1,0:T(8,128)S(1)} %terms_rim.1.own.rim_part, f32[2,16,4096]{2,1,0:T(8,128)S(1)} %terms_inner.1.inner_part, f32[32,256]{1,0:T(8,128)S(1)} %copy-done.4, f32[18,8,256]{2,1,0:T(8,128)S(1)} %collective-permute-done.pair, f32[17,8,256]{2,1,0:T(8,128)S(1)} %collective-permute-done.1.other, ...), custom_call_target="tpu_custom_call" | custom-call | bytes 8388608 | tf_op jit(solution)/shard_map/sketch/pallas_call | solution.py:463
  39.4 0.0 collective-permute-done.6.other
  39.4 0.0 collective-permute-done.5.pair
  39.4 0.5 gram.1
  39.9 0.1 collective-permute-start.7
  40.0 13.8 %all_to_all.11.grams = f32[32,8,128]{2,1,0:T(8,128)S(1)} all-to-all(f32[32,8,128]{2,1,0:T(8,128)S(1)} %get-tuple-element.30), channel_id=1, replica_groups=mesh['shot'=2,'strip'=16] {'shot','strip'}, dimensions={0} | all-to-all | bytes 262144 | tf_op jit(solution)/shard_map/all_to_all | solution.py:498
  53.8 0.0 collective-permute-done.7.theirs
  53.8 1.9 %factors.1 = (f32[16,32,256]{2,1,0:T(8,128)}, f32[16,32,256]{2,1,0:T(8,128)}) custom-call(f32[32,8,128]{2,1,0:T(8,128)S(1)} %all_to_all.11.grams, f32[16,8192]{1,0:T(8,128)S(1)} %get-tuple-element.31.own, f32[16,8192]{1,0:T(8,128)S(1)} %collective-permute-done.7.theirs), custom_call_target="tpu_custom_call" | custom-call | tf_op jit(solution)/shard_map/factors/pallas_call | solution.py:548
  (8 shorter events, 0.0 us)
Async XLA Ops:
  0.6 4.9 %copy-start.1 = (f32[1,64,32,256]{3,2,1,0:T(8,128)S(1)}, f32[1,64,32,256]{3,2,1,0:T(8,128)}, u32[]{:S(2)}) copy-start(f32[1,64,32,256]{3,2,1,0:T(8,128)} %param.10) | copy-start | bytes 6291460
  0.6 4.9 %copy-start = (f32[1,64,32,256]{3,2,1,0:T(8,128)S(1)}, f32[1,64,32,256]{3,2,1,0:T(8,128)}, u32[]{:S(2)}) copy-start(f32[1,64,32,256]{3,2,1,0:T(8,128)} %param.9) | copy-start | bytes 6291460
  0.7 4.9 %copy-start.3 = (f32[1,64,32,256]{3,2,1,0:T(8,128)S(1)}, f32[1,64,32,256]{3,2,1,0:T(8,128)}, u32[]{:S(2)}) copy-start(f32[1,64,32,256]{3,2,1,0:T(8,128)} %param.8) | copy-start | bytes 6291460
  0.7 4.9 %copy-start.2 = (f32[1,64,32,256]{3,2,1,0:T(8,128)S(1)}, f32[1,64,32,256]{3,2,1,0:T(8,128)}, u32[]{:S(2)}) copy-start(f32[1,64,32,256]{3,2,1,0:T(8,128)} %param.7) | copy-start | bytes 6291460
  1.9 8.6 %collective-permute-start = (f32[18,8,256]{2,1,0:T(8,128)S(1)}, f32[18,8,256]{2,1,0:T(8,128)S(1)}, u32[]{:S(2)}, u32[]{:S(2)}) collective-permute-start(f32[18,8,256]{2,1,0:T(8,128)S(1)} %get-tuple-element.17._), channel_id=1, source_target_pairs={{0,1},{1,0},{2,3},{3,2},{4,5},{5,4},{6,7},{7,6},{8,9},{9,8},{10,11... | collective-permute-start | bytes 442376 | tf_op jit(solution)/shard_map/ppermute | solution.py:147
  4.9 5.5 %collective-permute-start.1 = (f32[17,8,256]{2,1,0:T(8,128)S(1)}, f32[17,8,256]{2,1,0:T(8,128)S(1)}, u32[]{:S(2)}, u32[]{:S(2)}) collective-permute-start(f32[17,8,256]{2,1,0:T(8,128)S(1)} %get-tuple-element.22), channel_id=1, source_target_pairs={{1,2},{3,4},{5,6},{7,8},{9,10},{11,12},{13,14},{2,1},{4,3},{6,5},{... | collective-permute-start | bytes 417800 | tf_op jit(solution)/shard_map/ppermute | solution.py:146
  5.6 3.0 %copy-start.4 = (f32[32,256]{1,0:T(8,128)S(1)}, f32[32,256]{1,0:T(8,128)}, u32[]{:S(2)}) copy-start(f32[32,256]{1,0:T(8,128)} %speed.9) | copy-start | bytes 98308
  10.3 2.0 %collective-permute-start.3 = (f32[2,16,4096]{2,1,0:T(8,128)S(1)}, f32[2,16,4096]{2,1,0:T(8,128)S(1)}, u32[]{:S(2)}, u32[]{:S(2)}) collective-permute-start(f32[2,16,4096]{2,1,0:T(8,128)S(1)} %get-tuple-element.23.inner_mine), channel_id=1, source_target_pairs={{0,16},{16,0},{1,17},{17,1},{2,18},{18,2},{3,19},{19,3},{4,20},{20... | collective-permute-start | bytes 1572872 | tf_op jit(solution)/shard_map/ppermute | solution.py:242
  11.7 2.6 %collective-permute-start.2 = (f32[2,16,4096]{2,1,0:T(8,128)S(1)}, f32[2,16,4096]{2,1,0:T(8,128)S(1)}, u32[]{:S(2)}, u32[]{:S(2)}) collective-permute-start(f32[2,16,4096]{2,1,0:T(8,128)S(1)} %probes_rim.1.rim_mine), channel_id=1, source_target_pairs={{0,16},{16,0},{1,17},{17,1},{2,18},{18,2},{3,19},{19,3},{4,20},{20... | collective-permute-start | bytes 1572872 | tf_op jit(solution)/shard_map/ppermute | solution.py:288
  15.1 15.6 %collective-permute-start.4 = (f32[2,64,32,256]{3,2,1,0:T(8,128)S(1)}, f32[2,64,32,256]{3,2,1,0:T(8,128)S(1)}, u32[]{:S(2)}, u32[]{:S(2)}) collective-permute-start(f32[2,64,32,256]{3,2,1,0:T(8,128)S(1)} %get-tuple-element.27), channel_id=1, source_target_pairs={{0,16},{16,0},{1,17},{17,1},{2,18},{18,2},{3,19},{19,3},{4,20},{20... | collective-permute-start | bytes 12582920 | tf_op jit(solution)/shard_map/ppermute | solution.py:337
  33.3 6.1 %collective-permute-start.5 = (f32[16,2176]{1,0:T(8,128)S(1)}, f32[16,2176]{1,0:T(8,128)S(1)}, u32[]{:S(2)}, u32[]{:S(2)}) collective-permute-start(f32[16,2176]{1,0:T(8,128)S(1)} %get-tuple-element.28._), channel_id=1, source_target_pairs={{0,1},{1,0},{2,3},{3,2},{4,5},{5,4},{6,7},{7,6},{8,9},{9,8},{10,11... | collective-permute-start | bytes 417800 | tf_op jit(solution)/shard_map/ppermute | solution.py:421
  34.5 4.9 %collective-permute-start.6 = (f32[16,2048]{1,0:T(8,128)S(1)}, f32[16,2048]{1,0:T(8,128)S(1)}, u32[]{:S(2)}, u32[]{:S(2)}) collective-permute-start(f32[16,2048]{1,0:T(8,128)S(1)} %get-tuple-element.29), channel_id=1, source_target_pairs={{1,2},{3,4},{5,6},{7,8},{9,10},{11,12},{13,14},{2,1},{4,3},{6,5},{... | collective-permute-start | bytes 393224 | tf_op jit(solution)/shard_map/ppermute | solution.py:420
  39.9 13.8 %collective-permute-start.7 = (f32[16,8192]{1,0:T(8,128)S(1)}, f32[16,8192]{1,0:T(8,128)S(1)}, u32[]{:S(2)}, u32[]{:S(2)}) collective-permute-start(f32[16,8192]{1,0:T(8,128)S(1)} %get-tuple-element.31.own), channel_id=1, source_target_pairs={{0,16},{16,0},{1,17},{17,1},{2,18},{18,2},{3,19},{19,3},{4,20},{20... | collective-permute-start | bytes 1572872 | tf_op jit(solution)/shard_map/ppermute | solution.py:497

commit v3 on v2

--- a/solution.py
+++ b/solution.py
@@ -148,8 +148,8 @@
 
     group = math.gcd(waves, 16)
 
-    def lay_out(piece, out, high_at, low_at, at, t):
-        high, low = parts_of(jnp.swapaxes(piece, 0, 1), 2)
+    def lay_out(lines, out, high_at, low_at, at, t):
+        high, low = parts_of(lines, 2)
         for r in range(8):
             span = slice((at + r) * cols + t, (at + r) * cols + t + LANES)
             out[high_at, span] = high[r]
@@ -182,8 +182,9 @@
                 for block in range(0, rows, 8):
                     for t in range(0, cols, LANES):
                         span = slice(t, t + LANES)
-                        mine, other = adjoint[some, block : block + 8, span], source[some, block : block + 8, span]
-                        stage[level, some, block : block + 8, span] = jnp.where(side == 0, mine, other)
+                        mine = jnp.swapaxes(adjoint[some, block : block + 8, span], 0, 1)
+                        other = jnp.swapaxes(source[some, block : block + 8, span], 0, 1)
+                        stage[level, block : block + 8, some, span] = jnp.where(side == 0, mine, other)
                         lay_out(mine, out.at[0, level], some, low, block, t)
                         lay_out(other, out.at[1, level], some, low, block, t)
         speed_copy.wait()
@@ -197,7 +198,7 @@
         out_shape=[
             jax.ShapeDtypeStruct((2, 2, 2 * waves, cells), jnp.bfloat16),
             f32(rows, rank, cols),
-            f32(2, waves, rows, cols),
+            f32(2, rows, waves, cols),
         ],
         in_specs=[near] * 4 + [far] * 3 + [pl.BlockSpec(memory_space=pl.ANY)],
         out_specs=[near] * 3,
@@ -304,16 +305,6 @@
         )
         theirs[...] = products(fields_ref, inner_theirs, 1 - side, True)
 
-    def lay_out_raw(raw, blocks, out):
-        for level in range(2):
-            for first in range(0, waves, group):
-                some = slice(first, first + group)
-                low = slice(waves + first, waves + first + group)
-                for place, block in enumerate(blocks):
-                    for t in range(0, cols, LANES):
-                        piece = raw[level, some, block : block + 8, t : t + LANES]
-                        lay_out(piece, out.at[level], some, low, 8 * place, t)
-
     half = rank // 2
 
     def product_last_kernel(fields_ref, rim_theirs, mine_ref, theirs_ref, out):
@@ -337,7 +328,7 @@
     raw = lax.ppermute(stage, "shot", to_other)
     pieces = lax.all_to_all(pieces, ("shot", "strip"), 0, 0)
 
-    def combine(pieces_ref, fields_ref, swapped_ref, places, out):
+    def combine(pieces_ref, fields_ref, raw, blocks, out, swapped):
         side, _ = where_am_i()
         weights = []
         for shot in range(shots):
@@ -348,26 +339,25 @@
             stack = jnp.concatenate(parts_of(jnp.where(side == 0, own, other), 2), 0)
             stacks.append(jnp.concatenate([stack, stack], 1))
         for level in range(2):
-            for at, place, count in places:
+            for place, block in enumerate(blocks):
+                here = slice(block * cols, (block + 8) * cols)
+                there = slice(place * 8 * cols, (place + 1) * 8 * cols)
+                for r in range(8):
+                    high, low = parts_of(raw[level, block + r], 2)
+                    span = slice((place * 8 + r) * cols, (place * 8 + r + 1) * cols)
+                    swapped[level, :waves, span] = high
+                    swapped[level, waves:, span] = low
                 both = jnp.dot(
-                    stacks[0],
-                    fields_ref[1 - side, level, :, at : at + count],
-                    preferred_element_type=jnp.float32,
-                ) + jnp.dot(
-                    stacks[1],
-                    swapped_ref[level, :, place : place + count],
-                    preferred_element_type=jnp.float32,
-                )
-                out[level, :, place : place + count] = both[:rank] + both[rank:]
+                    stacks[0], fields_ref[1 - side, level, :, here], preferred_element_type=jnp.float32
+                ) + jnp.dot(stacks[1], swapped[level, :, there], preferred_element_type=jnp.float32)
+                out[level, :, there] = both[:rank] + both[rank:]
 
     def rim_terms_kernel(pieces_ref, fields_ref, raw, out, swapped):
-        lay_out_raw(raw, [*range(0, edge, 8), *range(rows - edge, rows, 8)], swapped)
-        places = [(0, 0, rim), (cells - rim, rim, rim)]
-        combine(pieces_ref, fields_ref, swapped, places, out)
+        blocks = [*range(0, edge, 8), *range(rows - edge, rows, 8)]
+        combine(pieces_ref, fields_ref, raw, blocks, out, swapped)
 
     def inner_terms_kernel(pieces_ref, fields_ref, raw, _, out, swapped):
-        lay_out_raw(raw, range(edge, rows - edge, 8), swapped)
-        combine(pieces_ref, fields_ref, swapped, [(rim, 0, inner * cols)], out)
+        combine(pieces_ref, fields_ref, raw, range(edge, rows - edge, 8), out, swapped)
 
     rim_terms = call(
         rim_terms_kernel,
@@ -379,7 +369,7 @@
     )(pieces, fields, raw)
 
     def spill_kernel(
-        own, speed, pair, other, pair_out, other_out,
+        own, speed, pair, other, pair_out, other_out, saved,
         up_now, up_prev, low_now, low_prev, up_speed, low_speed,
     ):
         _, even = where_am_i()
@@ -401,6 +391,9 @@
         for step in range(1, STEPS + 1):
             advance_rows(edge + 1 - step, 2 * edge + 1 - step, a, b, up_speed, False)
             advance_rows(step, edge + step, c, d, low_speed, False)
+            if step < STEPS:
+                saved[step - 1, :2] = b[2 * edge - 1 - step : 2 * edge + 1 - step]
+                saved[step - 1, 2:] = d[step : step + 2]
             a, b, c, d = b, a, d, c
         pair_out[:, rim:] = jnp.zeros((rank, LANES), jnp.float32)
         for r in range(edge):
@@ -410,9 +403,9 @@
             other_out[:, span] = jnp.where(even, upper, lower)
 
     spill = f32(rank, rim)
-    pair_spill, other_spill = call(
+    pair_spill, other_spill, spill_saved = call(
         spill_kernel,
-        [f32(rank, rim + LANES), spill],
+        [f32(rank, rim + LANES), spill, f32(STEPS - 1, 4, rank, cols)],
         16,
         [short] * 4 + [short_speed] * 2,
         name="spill",
@@ -428,61 +421,52 @@
         name="terms_inner",
         flops=flops,
     )(pieces, fields, raw, pair_spill)
-    pad = STEPS // 2 + 1
-    tall = rows + 2 * pad
-
-    def sketch_kernel(
-        rim_part, inner_part, speed, pair, other, _, out, now, prev, speeds
-    ):
-        above, below = far_speeds(pair, other)
-        speeds[:pad, :] = above[edge - pad :, :]
-        speeds[pad : pad + rows, :] = speed[...]
-        speeds[pad + rows :, :] = below[:pad, :]
-        zeros = jnp.zeros((pad, rank, cols), jnp.float32)
-        for ref in (now, prev):
-            ref[:pad] = zeros
-            ref[pad + rows :] = zeros
-        for r in range(rows):
+    def gram_of(piece):
+        stack = jnp.concatenate(parts_of(piece, 3), 0)
+        return dot32(stack, stack, NT)
+
+    def sketch_kernel(rim_part, inner_part, speed, saved, out, gram_out, now, prev, speeds):
+        speeds[1 : rows + 1, :] = speed[...]
+        for r in range(edge - 2, rows - edge + 2):
             part, line = rim_part, r
             if edge <= r < rows - edge:
                 part, line = inner_part, r - edge
             elif r >= edge:
                 line = r - inner
             span = slice(line * cols, (line + 1) * cols)
-            now[r + pad] = part[0, :, span]
-            prev[r + pad] = part[1, :, span]
+            now[r + 1] = part[0, :, span]
+            prev[r + 1] = part[1, :, span]
         a, b = now, prev
         for step in range(1, STEPS + 1):
-            reach = min(step, STEPS - step)
-            advance_rows(pad - reach, pad + rows + reach, a, b, speeds, False)
+            first, last = edge + 1 - step, rows - edge + 1 + step
+            advance_rows(first, last, a, b, speeds, False)
+            if step < STEPS:
+                b[first - 2 : first] = saved[step - 1, :2]
+                b[last : last + 2] = saved[step - 1, 2:]
             a, b = b, a
         for r in range(rows):
-            out[:, r * cols : (r + 1) * cols] = a[r + pad]
-
-    lines = pltpu.VMEM((tall, rank, cols), jnp.float32)
-    sketch_own = call(
+            out[:, r * cols : (r + 1) * cols] = a[r + 1]
+        gram_out[...] = gram_of(out[:, rim : cells - rim])
+
+    lines = pltpu.VMEM((rows + 2, rank, cols), jnp.float32)
+    sketch_own, inner_gram = call(
         sketch_kernel,
-        f32(rank, cells),
+        [f32(rank, cells), f32(3 * rank, 3 * rank)],
         16,
-        [lines, lines, pltpu.VMEM((tall, cols), jnp.float32)],
+        [lines, lines, pltpu.VMEM((rows + 2, cols), jnp.float32)],
         name="sketch",
         moved=8 * MIB,
-    )(rim_terms, inner_terms, courant, pair_halo, other_halo, pair_spill)
+    )(rim_terms, inner_terms, courant, spill_saved)
 
     places = shots * strips
 
-    def gram_kernel(own, pair, other, out, pieces_out):
+    def gram_kernel(own, pair, other, inner_total, out, pieces_out):
         _, even = where_am_i()
         top = own[:, :rim] + jnp.where(even, other[:, :rim], pair[:, :rim])
         bottom = own[:, cells - rim :] + jnp.where(even, pair[:, :rim], other[:, :rim])
-        middle = own[:, rim : cells - rim]
         out[:, :rim] = top
-        out[:, rim : cells - rim] = middle
         out[:, cells - rim :] = bottom
-        total = jnp.zeros((3 * rank, 3 * rank), jnp.float32)
-        for piece in (top, middle, bottom):
-            stack = jnp.concatenate(parts_of(piece, 3), 0)
-            total = total + dot32(stack, stack, NT)
+        total = inner_total[...] + gram_of(jnp.concatenate([top, bottom], 1))
         wide = total[:, :rank] + total[:, rank : 2 * rank] + total[:, 2 * rank :]
         gram = wide[:rank] + wide[rank : 2 * rank] + wide[2 * rank :]
         gram = jnp.concatenate(
@@ -491,14 +475,25 @@
         for place in range(places):
             pieces_out[place] = gram
 
-    sketch, gram_pieces = call(
-        gram_kernel, [f32(rank, cells), f32(places, rank // 2, LANES)], 12, name="gram"
-    )(sketch_own, pair_add, other_add)
+    sketch, gram_pieces = pl.pallas_call(
+        gram_kernel,
+        out_shape=[f32(rank, cells), f32(places, rank // 2, LANES)],
+        in_specs=[near] * 4,
+        out_specs=[near] * 2,
+        input_output_aliases={0: 0},
+        compiler_params=pltpu.CompilerParams(vmem_limit_bytes=12 * MIB),
+        name="gram",
+    )(sketch_own, pair_add, other_add, inner_gram)
     sketch_other = lax.ppermute(sketch, "shot", to_other)
     gram_pieces = lax.all_to_all(gram_pieces, ("shot", "strip"), 0, 0)
 
-    def factor_kernel(grams, own, theirs, left_out, right_out, held, sems):
+    def factor_kernel(grams, own, theirs, left_out, right_out, held, thick, sems):
         side, _ = where_am_i()
+        for shot in range(2):
+            for block in range(0, rows, 8):
+                span = slice(block * cols, (block + 8) * cols)
+                lines = jnp.where(side == shot, own[:, span], theirs[:, span])
+                thick[shot, :, span] = jnp.concatenate(parts_of(lines, 3), 0)
         line = lax.broadcasted_iota(jnp.int32, (rank, rank), 0)
         column = lax.broadcasted_iota(jnp.int32, (rank, rank), 1)
         tall_line = lax.broadcasted_iota(jnp.int32, (rank, LANES), 0)
@@ -525,9 +520,7 @@
             stack = jnp.concatenate([stack] * 3, 1)
             for block in range(0, rows, 8):
                 span = slice(block * cols, (block + 8) * cols)
-                lines = jnp.where(side == shot, own[:, span], theirs[:, span])
-                thick = jnp.concatenate(parts_of(lines, 3), 0)
-                solved = jnp.dot(stack, thick, preferred_element_type=jnp.float32)
+                solved = jnp.dot(stack, thick[shot, :, span], preferred_element_type=jnp.float32)
                 solved = solved[:rank] + solved[rank : 2 * rank] + solved[2 * rank :]
                 for t in range(0, cols, LANES):
                     tile = [solved[:, r * cols + t : r * cols + t + LANES][None] for r in range(8)]
@@ -552,6 +545,7 @@
         out_specs=[far] * 2,
         scratch_shapes=[
             pltpu.VMEM((2, rank, rows, cols), jnp.float32),
+            pltpu.VMEM((2, 3 * rank, cells), jnp.bfloat16),
             pltpu.SemaphoreType.DMA((2, rows // 8)),
         ],
         compiler_params=pltpu.CompilerParams(vmem_limit_bytes=12 * MIB),

time: 56 us -> 55.4 us (0.989)
  Pallas kernels: 19 us -> 17 us
  waiting for transfers between devices: 0.14 us -> 1.08 us
    ppermute x1, waiting for transfers between devices: 0.01 us -> 0.94 us  [shards(): pair_add = lax.ppermute(pair_spill, 'strip', to_pair)]
    pallas_call x1, Pallas kernels: 1.51 us -> 0.82 us  [shards(): call(inner_terms_kernel, f32(2, rank, inner * cols), 24, [pltpu.VMEM((2,...]
    pallas_call x1, Pallas kernels: 1.5 us -> 0.82 us  [shards(): call(rim_terms_kernel, f32(2, rank, 2 * rim), 24, [pltpu.VMEM((2, 2 * wav...]
    pallas_call x3, Pallas kernels: 4.14 us -> 3.5 us  [the longest x1 1.87 us: shards(): call(sketch_kernel, [f32(rank, cells), f32(3 * rank, 3 * rank)], 16, [lin...]
  transfers between devices with their start and end apart: 8 -> 8, of which waited for: 1 -> 2; matrix products, arithmetic and copies ran while one was open for 0% -> 0% of each run, Pallas kernels for 21% -> 19%
where the time goes in v3:
time: 55.4 us; the launch traced here: 55.2 us
  blocking collectives  29.5 us (53%)
  Pallas kernels  17 us (31%)
  starting transfers between devices  6.6 us (12%)
  waiting for transfers between devices  1.08 us (2%)
  between operations  0.99 us (2%)
    all_to_all x1, blocking collectives, shards(): pieces = lax.all_to_all(pieces, ('shot', 'strip'), 0, 0)  15.3 us
    all_to_all x1, blocking collectives, shards(): gram_pieces = lax.all_to_all(gram_pieces, ('shot', 'strip'), 0, 0)  14.2 us
    pallas_call x1, Pallas kernels, shards(): pl.pallas_call(split_kernel, out_shape=[jax.ShapeDtypeStruct((2, 2, 2 * w...  3.16 us
    ppermute x1, starting transfers between devices, shards(): pair_halo = lax.ppermute(pair_edge, 'strip', to_pair)  3 us
    pallas_call x1, Pallas kernels, shards(): call(product_kernel, [f32(rank, waves)] * 2, 24, name='product')  1.89 us
    pallas_call x1, Pallas kernels, shards(): pl.pallas_call(factor_kernel, out_shape=[factor, factor], in_specs=[near]...  1.88 us
    pallas_call x1, Pallas kernels, shards(): call(sketch_kernel, [f32(rank, cells), f32(3 * rank, 3 * rank)], 16, [lin...  1.87 us
    pallas_call x1, Pallas kernels, shards(): call(inner_kernel, [f32(2, rank, inner * cols), f32(STEPS, 4, rank, cols)...  1.66 us
  transfers between devices with their start and end apart: 8, of which 2 were waited for; matrix products, arithmetic and copies ran while one was open for 0% of the time, Pallas kernels for 19%

profile of v3, /device:TPU:0, one launch (start us, length us, event | category | flops | bytes accessed | tf_op | source)
XLA Modules:
  0.0 55.2 jit_solution(95493967439729565)
XLA Ops:
  0.6 0.0 copy-start.1
  0.7 1.2 %edges.1 = (f32[18,8,256]{2,1,0:T(8,128)S(1)}, f32[17,8,256]{2,1,0:T(8,128)S(1)}) custom-call(f32[16,32,256]{2,1,0:T(8,128)} %left.3, f32[16,32,256]{2,1,0:T(8,128)} %right.3, f32[32,256]{1,0:T(8,128)} %speed.9), custom_call_target="tpu_custom_call" | custom-call | flops 20000000000 | bytes 4194304 | tf_op jit(solution)/shard_map/edges/pallas_call | solution.py:136
  1.9 3.0 %collective-permute-start = (f32[18,8,256]{2,1,0:T(8,128)S(1)}, f32[18,8,256]{2,1,0:T(8,128)S(1)}, u32[]{:S(2)}, u32[]{:S(2)}) collective-permute-start(f32[18,8,256]{2,1,0:T(8,128)S(1)} %get-tuple-element.20._), channel_id=1, source_target_pairs={{0,1},{1,0},{2,3},{3,2},{4,5},{5,4},{6,7},{7,6},{8,9},{9,8},{10,11... | collective-permute-start | bytes 442376 | tf_op jit(solution)/shard_map/ppermute | solution.py:147
  4.9 0.7 %collective-permute-start.1 = (f32[17,8,256]{2,1,0:T(8,128)S(1)}, f32[17,8,256]{2,1,0:T(8,128)S(1)}, u32[]{:S(2)}, u32[]{:S(2)}) collective-permute-start(f32[17,8,256]{2,1,0:T(8,128)S(1)} %get-tuple-element.25), channel_id=1, source_target_pairs={{1,2},{3,4},{5,6},{7,8},{9,10},{11,12},{13,14},{2,1},{4,3},{6,5},{... | collective-permute-start | bytes 417800 | tf_op jit(solution)/shard_map/ppermute | solution.py:146
  5.6 0.0 copy-start.4
  5.6 3.2 %split.1 = (bf16[2,2,128,8192]{3,2,1,0:T(8,128)(2,1)S(1)}, f32[32,16,256]{2,1,0:T(8,128)S(1)}, f32[2,32,64,256]{3,2,1,0:T(8,128)S(1)}) custom-call(f32[64,32,256]{2,1,0:T(8,128)S(1)} %bitcast.4, f32[64,32,256]{2,1,0:T(8,128)S(1)} %bitcast.5, f32[64,32,256]{2,1,0:T(8,128)S(1)} %bitcast.6, f32[64,32,256]{2,1,0:T(8,128)S(1)} %bitcast.7, f32[16,32,256]{2,1,0:T(8,128)} %left.3, ...), custom_call_target="tpu_custom_call" | custom-call | bytes 16777216 | tf_op jit(solution)/shard_map/split/pallas_call | solution.py:196
  8.8 1.7 %probes_inner.1 = (f32[2,16,4096]{2,1,0:T(8,128)S(1)}, f32[8,4,16,256]{3,2,1,0:T(8,128)S(1)}) custom-call(f32[32,16,256]{2,1,0:T(8,128)S(1)} %get-tuple-element.23.begin, f32[32,256]{1,0:T(8,128)S(1)} %copy-done.4), custom_call_target="tpu_custom_call" | custom-call | tf_op jit(solution)/shard_map/probes_inner/pallas_call | solution.py:236
  10.5 0.1 collective-permute-start.3
  10.5 0.0 collective-permute-done.1.other
  10.5 0.0 collective-permute-done.pair
  10.6 1.2 %probes_rim.1.rim_mine = f32[2,16,4096]{2,1,0:T(8,128)S(1)} custom-call(f32[8,4,16,256]{3,2,1,0:T(8,128)S(1)} %get-tuple-element.24.saved, f32[32,256]{1,0:T(8,128)S(1)} %copy-done.4, f32[18,8,256]{2,1,0:T(8,128)S(1)} %collective-permute-done.pair, f32[17,8,256]{2,1,0:T(8,128)S(1)} %collective-permute-done.1.other), custom_call_target="tpu_custom_call" | custom-call | tf_op jit(solution)/shard_map/probes_rim/pallas_call | solution.py:282
  11.8 0.5 collective-permute-start.2
  12.3 0.1 collective-permute-done.3.inner_theirs
  12.4 1.9 %product.1 = (f32[16,64]{1,0:T(8,128)S(1)}, f32[16,64]{1,0:T(8,128)S(1)}) custom-call(bf16[2,2,128,8192]{3,2,1,0:T(8,128)(2,1)S(1)} %get-tuple-element.22.fields_ref, f32[2,16,4096]{2,1,0:T(8,128)S(1)} %get-tuple-element.26.inner_mine, f32[2,16,4096]{2,1,0:T(8,128)S(1)} %collective-permute-done.3.inner_theirs, f32[2,16,4096]{2,1,0:T(8,128)S(1)} %probes_rim.1.rim_mine), custom_call_target="tpu_custom_call" | custom-call | tf_op jit(solution)/shard_map/product/pallas_call | solution.py:321
  14.3 0.0 collective-permute-done.2.rim_theirs
  14.3 0.9 %product_last.1 = f32[32,8,128]{2,1,0:T(8,128)S(1)} custom-call(bf16[2,2,128,8192]{3,2,1,0:T(8,128)(2,1)S(1)} %get-tuple-element.22.fields_ref, f32[2,16,4096]{2,1,0:T(8,128)S(1)} %collective-permute-done.2.rim_theirs, f32[16,64]{1,0:T(8,128)S(1)} %get-tuple-element.27.mine_ref, f32[16,64]{1,0:T(8,128)S(1)} %get-tuple-element.28.theirs_ref), custom_call_target="tpu_custom_call" | custom-call | tf_op jit(solution)/shard_map/product_last/pallas_call | solution.py:324
  15.2 0.2 collective-permute-start.4
  15.4 15.3 %all_to_all.10.pieces_ref = f32[32,8,128]{2,1,0:T(8,128)S(1)} all-to-all(f32[32,8,128]{2,1,0:T(8,128)S(1)} %product_last.1), channel_id=1, replica_groups=mesh['shot'=2,'strip'=16] {'shot','strip'}, dimensions={0} | all-to-all | bytes 262144 | tf_op jit(solution)/shard_map/all_to_all | solution.py:329
  30.8 0.0 collective-permute-done.4.raw
  30.8 0.8 %terms_rim.1.own.rim_part = f32[2,16,4096]{2,1,0:T(8,128)S(1)} custom-call(f32[32,8,128]{2,1,0:T(8,128)S(1)} %all_to_all.10.pieces_ref, bf16[2,2,128,8192]{3,2,1,0:T(8,128)(2,1)S(1)} %get-tuple-element.22.fields_ref, f32[2,32,64,256]{3,2,1,0:T(8,128)S(1)} %collective-permute-done.4.raw), custom_call_target="tpu_custom_call" | custom-call | flops 134217728 | tf_op jit(solution)/shard_map/terms_rim/pallas_call | solution.py:362
  31.6 1.1 %spill.1 = (f32[16,2176]{1,0:T(8,128)S(1)}, f32[16,2048]{1,0:T(8,128)S(1)}, f32[7,4,16,256]{3,2,1,0:T(8,128)S(1)}) custom-call(f32[2,16,4096]{2,1,0:T(8,128)S(1)} %terms_rim.1.own.rim_part, f32[32,256]{1,0:T(8,128)S(1)} %copy-done.4, f32[18,8,256]{2,1,0:T(8,128)S(1)} %collective-permute-done.pair, f32[17,8,256]{2,1,0:T(8,128)S(1)} %collective-permute-done.1.other), custom_call_target="tpu_custom_call" | custom-call | tf_op jit(solution)/shard_map/spill/pallas_call | solution.py:406
  32.7 1.2 %collective-permute-start.5 = (f32[16,2176]{1,0:T(8,128)S(1)}, f32[16,2176]{1,0:T(8,128)S(1)}, u32[]{:S(2)}, u32[]{:S(2)}) collective-permute-start(f32[16,2176]{1,0:T(8,128)S(1)} %get-tuple-element.31._), channel_id=1, source_target_pairs={{0,1},{1,0},{2,3},{3,2},{4,5},{5,4},{6,7},{7,6},{8,9},{9,8},{10,11... | collective-permute-start | bytes 417800 | tf_op jit(solution)/shard_map/ppermute | solution.py:414
  33.9 0.8 %collective-permute-start.6 = (f32[16,2048]{1,0:T(8,128)S(1)}, f32[16,2048]{1,0:T(8,128)S(1)}, u32[]{:S(2)}, u32[]{:S(2)}) collective-permute-start(f32[16,2048]{1,0:T(8,128)S(1)} %get-tuple-element.34), channel_id=1, source_target_pairs={{1,2},{3,4},{5,6},{7,8},{9,10},{11,12},{13,14},{2,1},{4,3},{6,5},{... | collective-permute-start | bytes 393224 | tf_op jit(solution)/shard_map/ppermute | solution.py:413
  34.8 0.8 %terms_inner.1.inner_part = f32[2,16,4096]{2,1,0:T(8,128)S(1)} custom-call(f32[32,8,128]{2,1,0:T(8,128)S(1)} %all_to_all.10.pieces_ref, bf16[2,2,128,8192]{3,2,1,0:T(8,128)(2,1)S(1)} %get-tuple-element.22.fields_ref, f32[2,32,64,256]{3,2,1,0:T(8,128)S(1)} %collective-permute-done.4.raw, f32[16,2176]{1,0:T(8,128)S(1)} %get-tuple-element.31._), custom_call_target="tpu_custom_call" | custom-call | flops 134217728 | tf_op jit(solution)/shard_map/terms_inner/pallas_call | solution.py:416
  35.6 1.9 %sketch.1 = (f32[16,8192]{1,0:T(8,128)S(1)}, f32[48,48]{1,0:T(8,128)S(1)}) custom-call(f32[2,16,4096]{2,1,0:T(8,128)S(1)} %terms_rim.1.own.rim_part, f32[2,16,4096]{2,1,0:T(8,128)S(1)} %terms_inner.1.inner_part, f32[32,256]{1,0:T(8,128)S(1)} %copy-done.4, f32[7,4,16,256]{3,2,1,0:T(8,128)S(1)} %get-tuple-element.32.saved), custom_call_target="tpu_custom_call" | custom-call | bytes 8388608 | tf_op jit(solution)/shard_map/sketch/pallas_call | solution.py:452
  37.5 0.0 collective-permute-done.6.other
  37.5 0.9 %collective-permute-done.5.pair = f32[16,2176]{1,0:T(8,128)S(1)} collective-permute-done((f32[16,2176]{1,0:T(8,128)S(1)}, f32[16,2176]{1,0:T(8,128)S(1)}, u32[]{:S(2)}, u32[]{:S(2)}) %collective-permute-start.5) | collective-permute-done | bytes 139296 | tf_op jit(solution)/shard_map/ppermute | solution.py:414
  38.4 0.5 gram.1
  39.0 0.1 collective-permute-start.7
  39.0 14.2 %all_to_all.11.grams = f32[32,8,128]{2,1,0:T(8,128)S(1)} all-to-all(f32[32,8,128]{2,1,0:T(8,128)S(1)} %get-tuple-element.36), channel_id=1, replica_groups=mesh['shot'=2,'strip'=16] {'shot','strip'}, dimensions={0} | all-to-all | bytes 262144 | tf_op jit(solution)/shard_map/all_to_all | solution.py:488
  53.2 0.0 collective-permute-done.7.theirs
  53.2 1.9 %factors.1 = (f32[16,32,256]{2,1,0:T(8,128)}, f32[16,32,256]{2,1,0:T(8,128)}) custom-call(f32[32,8,128]{2,1,0:T(8,128)S(1)} %all_to_all.11.grams, f32[16,8192]{1,0:T(8,128)S(1)} %get-tuple-element.37.own, f32[16,8192]{1,0:T(8,128)S(1)} %collective-permute-done.7.theirs), custom_call_target="tpu_custom_call" | custom-call | tf_op jit(solution)/shard_map/factors/pallas_call | solution.py:541
  (8 shorter events, 0.0 us)
Async XLA Ops:
  0.6 4.9 %copy-start.1 = (f32[1,64,32,256]{3,2,1,0:T(8,128)S(1)}, f32[1,64,32,256]{3,2,1,0:T(8,128)}, u32[]{:S(2)}) copy-start(f32[1,64,32,256]{3,2,1,0:T(8,128)} %param.10) | copy-start | bytes 6291460
  0.6 4.9 %copy-start = (f32[1,64,32,256]{3,2,1,0:T(8,128)S(1)}, f32[1,64,32,256]{3,2,1,0:T(8,128)}, u32[]{:S(2)}) copy-start(f32[1,64,32,256]{3,2,1,0:T(8,128)} %param.9) | copy-start | bytes 6291460
  0.7 4.9 %copy-start.3 = (f32[1,64,32,256]{3,2,1,0:T(8,128)S(1)}, f32[1,64,32,256]{3,2,1,0:T(8,128)}, u32[]{:S(2)}) copy-start(f32[1,64,32,256]{3,2,1,0:T(8,128)} %param.8) | copy-start | bytes 6291460
  0.7 4.9 %copy-start.2 = (f32[1,64,32,256]{3,2,1,0:T(8,128)S(1)}, f32[1,64,32,256]{3,2,1,0:T(8,128)}, u32[]{:S(2)}) copy-start(f32[1,64,32,256]{3,2,1,0:T(8,128)} %param.7) | copy-start | bytes 6291460
  1.9 8.7 %collective-permute-start = (f32[18,8,256]{2,1,0:T(8,128)S(1)}, f32[18,8,256]{2,1,0:T(8,128)S(1)}, u32[]{:S(2)}, u32[]{:S(2)}) collective-permute-start(f32[18,8,256]{2,1,0:T(8,128)S(1)} %get-tuple-element.20._), channel_id=1, source_target_pairs={{0,1},{1,0},{2,3},{3,2},{4,5},{5,4},{6,7},{7,6},{8,9},{9,8},{10,11... | collective-permute-start | bytes 442376 | tf_op jit(solution)/shard_map/ppermute | solution.py:147
  4.9 5.6 %collective-permute-start.1 = (f32[17,8,256]{2,1,0:T(8,128)S(1)}, f32[17,8,256]{2,1,0:T(8,128)S(1)}, u32[]{:S(2)}, u32[]{:S(2)}) collective-permute-start(f32[17,8,256]{2,1,0:T(8,128)S(1)} %get-tuple-element.25), channel_id=1, source_target_pairs={{1,2},{3,4},{5,6},{7,8},{9,10},{11,12},{13,14},{2,1},{4,3},{6,5},{... | collective-permute-start | bytes 417800 | tf_op jit(solution)/shard_map/ppermute | solution.py:146
  5.6 3.2 %copy-start.4 = (f32[32,256]{1,0:T(8,128)S(1)}, f32[32,256]{1,0:T(8,128)}, u32[]{:S(2)}) copy-start(f32[32,256]{1,0:T(8,128)} %speed.9) | copy-start | bytes 98308
  10.5 2.0 %collective-permute-start.3 = (f32[2,16,4096]{2,1,0:T(8,128)S(1)}, f32[2,16,4096]{2,1,0:T(8,128)S(1)}, u32[]{:S(2)}, u32[]{:S(2)}) collective-permute-start(f32[2,16,4096]{2,1,0:T(8,128)S(1)} %get-tuple-element.26.inner_mine), channel_id=1, source_target_pairs={{0,16},{16,0},{1,17},{17,1},{2,18},{18,2},{3,19},{19,3},{4,20},{20... | collective-permute-start | bytes 1572872 | tf_op jit(solution)/shard_map/ppermute | solution.py:243
  11.8 2.6 %collective-permute-start.2 = (f32[2,16,4096]{2,1,0:T(8,128)S(1)}, f32[2,16,4096]{2,1,0:T(8,128)S(1)}, u32[]{:S(2)}, u32[]{:S(2)}) collective-permute-start(f32[2,16,4096]{2,1,0:T(8,128)S(1)} %probes_rim.1.rim_mine), channel_id=1, source_target_pairs={{0,16},{16,0},{1,17},{17,1},{2,18},{18,2},{3,19},{19,3},{4,20},{20... | collective-permute-start | bytes 1572872 | tf_op jit(solution)/shard_map/ppermute | solution.py:289
  15.2 15.5 %collective-permute-start.4 = (f32[2,32,64,256]{3,2,1,0:T(8,128)S(1)}, f32[2,32,64,256]{3,2,1,0:T(8,128)S(1)}, u32[]{:S(2)}, u32[]{:S(2)}) collective-permute-start(f32[2,32,64,256]{3,2,1,0:T(8,128)S(1)} %get-tuple-element.30), channel_id=1, source_target_pairs={{0,16},{16,0},{1,17},{17,1},{2,18},{18,2},{3,19},{19,3},{4,20},{20... | collective-permute-start | bytes 12582920 | tf_op jit(solution)/shard_map/ppermute | solution.py:328
  32.7 5.7 %collective-permute-start.5 = (f32[16,2176]{1,0:T(8,128)S(1)}, f32[16,2176]{1,0:T(8,128)S(1)}, u32[]{:S(2)}, u32[]{:S(2)}) collective-permute-start(f32[16,2176]{1,0:T(8,128)S(1)} %get-tuple-element.31._), channel_id=1, source_target_pairs={{0,1},{1,0},{2,3},{3,2},{4,5},{5,4},{6,7},{7,6},{8,9},{9,8},{10,11... | collective-permute-start | bytes 417800 | tf_op jit(solution)/shard_map/ppermute | solution.py:414
  33.9 3.6 %collective-permute-start.6 = (f32[16,2048]{1,0:T(8,128)S(1)}, f32[16,2048]{1,0:T(8,128)S(1)}, u32[]{:S(2)}, u32[]{:S(2)}) collective-permute-start(f32[16,2048]{1,0:T(8,128)S(1)} %get-tuple-element.34), channel_id=1, source_target_pairs={{1,2},{3,4},{5,6},{7,8},{9,10},{11,12},{13,14},{2,1},{4,3},{6,5},{... | collective-permute-start | bytes 393224 | tf_op jit(solution)/shard_map/ppermute | solution.py:413
  39.0 14.2 %collective-permute-start.7 = (f32[16,8192]{1,0:T(8,128)S(1)}, f32[16,8192]{1,0:T(8,128)S(1)}, u32[]{:S(2)}, u32[]{:S(2)}) collective-permute-start(f32[16,8192]{1,0:T(8,128)S(1)} %get-tuple-element.37.own), channel_id=1, source_target_pairs={{0,16},{16,0},{1,17},{17,1},{2,18},{18,2},{3,19},{19,3},{4,20},{20... | collective-permute-start | bytes 1572872 | tf_op jit(solution)/shard_map/ppermute | solution.py:487

commit v4 on v3

--- a/solution.py
+++ b/solution.py
@@ -493,7 +493,7 @@
             for block in range(0, rows, 8):
                 span = slice(block * cols, (block + 8) * cols)
                 lines = jnp.where(side == shot, own[:, span], theirs[:, span])
-                thick[shot, :, span] = jnp.concatenate(parts_of(lines, 3), 0)
+                thick[shot, :, span] = jnp.concatenate(parts_of(lines, 2), 0)
         line = lax.broadcasted_iota(jnp.int32, (rank, rank), 0)
         column = lax.broadcasted_iota(jnp.int32, (rank, rank), 1)
         tall_line = lax.broadcasted_iota(jnp.int32, (rank, LANES), 0)
@@ -516,12 +516,12 @@
             for j in range(1, rank):
                 pivots = jnp.where(tall_line == j, columns[j], pivots)
             inverse = inverse[0] * (lax.rsqrt(pivots[:, :rank]) * factor_scale)
-            stack = jnp.concatenate(parts_of(inverse, 3), 0)
-            stack = jnp.concatenate([stack] * 3, 1)
+            stack = jnp.concatenate(parts_of(inverse, 2), 0)
+            stack = jnp.concatenate([stack] * 2, 1)
             for block in range(0, rows, 8):
                 span = slice(block * cols, (block + 8) * cols)
                 solved = jnp.dot(stack, thick[shot, :, span], preferred_element_type=jnp.float32)
-                solved = solved[:rank] + solved[rank : 2 * rank] + solved[2 * rank :]
+                solved = solved[:rank] + solved[rank:]
                 for t in range(0, cols, LANES):
                     tile = [solved[:, r * cols + t : r * cols + t + LANES][None] for r in range(8)]
                     held[shot, :, block : block + 8, t : t + LANES] = jnp.swapaxes(
@@ -545,7 +545,7 @@
         out_specs=[far] * 2,
         scratch_shapes=[
             pltpu.VMEM((2, rank, rows, cols), jnp.float32),
-            pltpu.VMEM((2, 3 * rank, cells), jnp.bfloat16),
+            pltpu.VMEM((2, 2 * rank, cells), jnp.bfloat16),
             pltpu.SemaphoreType.DMA((2, rows // 8)),
         ],
         compiler_params=pltpu.CompilerParams(vmem_limit_bytes=12 * MIB),

time: 55.4 us -> 55.2 us (level)
  no operation moved by 1% of the time
where the time goes in v4:
time: 55.2 us; the launch traced here: 55 us
  blocking collectives  29.5 us (53%)
  Pallas kernels  16.8 us (30%)
  starting transfers between devices  6.6 us (12%)
  waiting for transfers between devices  1.08 us (2%)
  between operations  0.99 us (2%)
    all_to_all x1, blocking collectives, shards(): pieces = lax.all_to_all(pieces, ('shot', 'strip'), 0, 0)  15.3 us
    all_to_all x1, blocking collectives, shards(): gram_pieces = lax.all_to_all(gram_pieces, ('shot', 'strip'), 0, 0)  14.2 us
    pallas_call x1, Pallas kernels, shards(): pl.pallas_call(split_kernel, out_shape=[jax.ShapeDtypeStruct((2, 2, 2 * w...  3.16 us
    ppermute x1, starting transfers between devices, shards(): pair_halo = lax.ppermute(pair_edge, 'strip', to_pair)  3 us
    pallas_call x1, Pallas kernels, shards(): call(product_kernel, [f32(rank, waves)] * 2, 24, name='product')  1.89 us
    pallas_call x1, Pallas kernels, shards(): call(sketch_kernel, [f32(rank, cells), f32(3 * rank, 3 * rank)], 16, [lin...  1.87 us
    pallas_call x1, Pallas kernels, shards(): pl.pallas_call(factor_kernel, out_shape=[factor, factor], in_specs=[near]...  1.7 us
    pallas_call x1, Pallas kernels, shards(): call(inner_kernel, [f32(2, rank, inner * cols), f32(STEPS, 4, rank, cols)...  1.66 us
  transfers between devices with their start and end apart: 8, of which 2 were waited for; matrix products, arithmetic and copies ran while one was open for 0% of the time, Pallas kernels for 19%

profile of v4, /device:TPU:0, one launch (start us, length us, event | category | flops | bytes accessed | tf_op | source)
XLA Modules:
  0.0 55.0 jit_solution(10428169725765908982)
XLA Ops:
  0.6 0.0 copy-start.1
  0.7 1.2 %edges.1 = (f32[18,8,256]{2,1,0:T(8,128)S(1)}, f32[17,8,256]{2,1,0:T(8,128)S(1)}) custom-call(f32[16,32,256]{2,1,0:T(8,128)} %left.3, f32[16,32,256]{2,1,0:T(8,128)} %right.3, f32[32,256]{1,0:T(8,128)} %speed.9), custom_call_target="tpu_custom_call" | custom-call | flops 20000000000 | bytes 4194304 | tf_op jit(solution)/shard_map/edges/pallas_call | solution.py:136
  1.9 3.0 %collective-permute-start = (f32[18,8,256]{2,1,0:T(8,128)S(1)}, f32[18,8,256]{2,1,0:T(8,128)S(1)}, u32[]{:S(2)}, u32[]{:S(2)}) collective-permute-start(f32[18,8,256]{2,1,0:T(8,128)S(1)} %get-tuple-element.20._), channel_id=1, source_target_pairs={{0,1},{1,0},{2,3},{3,2},{4,5},{5,4},{6,7},{7,6},{8,9},{9,8},{10,11... | collective-permute-start | bytes 442376 | tf_op jit(solution)/shard_map/ppermute | solution.py:147
  4.9 0.7 %collective-permute-start.1 = (f32[17,8,256]{2,1,0:T(8,128)S(1)}, f32[17,8,256]{2,1,0:T(8,128)S(1)}, u32[]{:S(2)}, u32[]{:S(2)}) collective-permute-start(f32[17,8,256]{2,1,0:T(8,128)S(1)} %get-tuple-element.25), channel_id=1, source_target_pairs={{1,2},{3,4},{5,6},{7,8},{9,10},{11,12},{13,14},{2,1},{4,3},{6,5},{... | collective-permute-start | bytes 417800 | tf_op jit(solution)/shard_map/ppermute | solution.py:146
  5.6 0.0 copy-start.4
  5.6 3.2 %split.1 = (bf16[2,2,128,8192]{3,2,1,0:T(8,128)(2,1)S(1)}, f32[32,16,256]{2,1,0:T(8,128)S(1)}, f32[2,32,64,256]{3,2,1,0:T(8,128)S(1)}) custom-call(f32[64,32,256]{2,1,0:T(8,128)S(1)} %bitcast.4, f32[64,32,256]{2,1,0:T(8,128)S(1)} %bitcast.5, f32[64,32,256]{2,1,0:T(8,128)S(1)} %bitcast.6, f32[64,32,256]{2,1,0:T(8,128)S(1)} %bitcast.7, f32[16,32,256]{2,1,0:T(8,128)} %left.3, ...), custom_call_target="tpu_custom_call" | custom-call | bytes 16777216 | tf_op jit(solution)/shard_map/split/pallas_call | solution.py:196
  8.8 1.7 %probes_inner.1 = (f32[2,16,4096]{2,1,0:T(8,128)S(1)}, f32[8,4,16,256]{3,2,1,0:T(8,128)S(1)}) custom-call(f32[32,16,256]{2,1,0:T(8,128)S(1)} %get-tuple-element.23.begin, f32[32,256]{1,0:T(8,128)S(1)} %copy-done.4), custom_call_target="tpu_custom_call" | custom-call | tf_op jit(solution)/shard_map/probes_inner/pallas_call | solution.py:236
  10.5 0.1 collective-permute-start.3
  10.5 0.0 collective-permute-done.1.other
  10.5 0.0 collective-permute-done.pair
  10.6 1.2 %probes_rim.1.rim_mine = f32[2,16,4096]{2,1,0:T(8,128)S(1)} custom-call(f32[8,4,16,256]{3,2,1,0:T(8,128)S(1)} %get-tuple-element.24.saved, f32[32,256]{1,0:T(8,128)S(1)} %copy-done.4, f32[18,8,256]{2,1,0:T(8,128)S(1)} %collective-permute-done.pair, f32[17,8,256]{2,1,0:T(8,128)S(1)} %collective-permute-done.1.other), custom_call_target="tpu_custom_call" | custom-call | tf_op jit(solution)/shard_map/probes_rim/pallas_call | solution.py:282
  11.8 0.5 collective-permute-start.2
  12.3 0.1 collective-permute-done.3.inner_theirs
  12.4 1.9 %product.1 = (f32[16,64]{1,0:T(8,128)S(1)}, f32[16,64]{1,0:T(8,128)S(1)}) custom-call(bf16[2,2,128,8192]{3,2,1,0:T(8,128)(2,1)S(1)} %get-tuple-element.22.fields_ref, f32[2,16,4096]{2,1,0:T(8,128)S(1)} %get-tuple-element.26.inner_mine, f32[2,16,4096]{2,1,0:T(8,128)S(1)} %collective-permute-done.3.inner_theirs, f32[2,16,4096]{2,1,0:T(8,128)S(1)} %probes_rim.1.rim_mine), custom_call_target="tpu_custom_call" | custom-call | tf_op jit(solution)/shard_map/product/pallas_call | solution.py:321
  14.3 0.0 collective-permute-done.2.rim_theirs
  14.3 0.9 %product_last.1 = f32[32,8,128]{2,1,0:T(8,128)S(1)} custom-call(bf16[2,2,128,8192]{3,2,1,0:T(8,128)(2,1)S(1)} %get-tuple-element.22.fields_ref, f32[2,16,4096]{2,1,0:T(8,128)S(1)} %collective-permute-done.2.rim_theirs, f32[16,64]{1,0:T(8,128)S(1)} %get-tuple-element.27.mine_ref, f32[16,64]{1,0:T(8,128)S(1)} %get-tuple-element.28.theirs_ref), custom_call_target="tpu_custom_call" | custom-call | tf_op jit(solution)/shard_map/product_last/pallas_call | solution.py:324
  15.2 0.2 collective-permute-start.4
  15.4 15.3 %all_to_all.10.pieces_ref = f32[32,8,128]{2,1,0:T(8,128)S(1)} all-to-all(f32[32,8,128]{2,1,0:T(8,128)S(1)} %product_last.1), channel_id=1, replica_groups=mesh['shot'=2,'strip'=16] {'shot','strip'}, dimensions={0} | all-to-all | bytes 262144 | tf_op jit(solution)/shard_map/all_to_all | solution.py:329
  30.8 0.0 collective-permute-done.4.raw
  30.8 0.8 %terms_rim.1.own.rim_part = f32[2,16,4096]{2,1,0:T(8,128)S(1)} custom-call(f32[32,8,128]{2,1,0:T(8,128)S(1)} %all_to_all.10.pieces_ref, bf16[2,2,128,8192]{3,2,1,0:T(8,128)(2,1)S(1)} %get-tuple-element.22.fields_ref, f32[2,32,64,256]{3,2,1,0:T(8,128)S(1)} %collective-permute-done.4.raw), custom_call_target="tpu_custom_call" | custom-call | flops 134217728 | tf_op jit(solution)/shard_map/terms_rim/pallas_call | solution.py:362
  31.6 1.1 %spill.1 = (f32[16,2176]{1,0:T(8,128)S(1)}, f32[16,2048]{1,0:T(8,128)S(1)}, f32[7,4,16,256]{3,2,1,0:T(8,128)S(1)}) custom-call(f32[2,16,4096]{2,1,0:T(8,128)S(1)} %terms_rim.1.own.rim_part, f32[32,256]{1,0:T(8,128)S(1)} %copy-done.4, f32[18,8,256]{2,1,0:T(8,128)S(1)} %collective-permute-done.pair, f32[17,8,256]{2,1,0:T(8,128)S(1)} %collective-permute-done.1.other), custom_call_target="tpu_custom_call" | custom-call | tf_op jit(solution)/shard_map/spill/pallas_call | solution.py:406
  32.7 1.2 %collective-permute-start.5 = (f32[16,2176]{1,0:T(8,128)S(1)}, f32[16,2176]{1,0:T(8,128)S(1)}, u32[]{:S(2)}, u32[]{:S(2)}) collective-permute-start(f32[16,2176]{1,0:T(8,128)S(1)} %get-tuple-element.31._), channel_id=1, source_target_pairs={{0,1},{1,0},{2,3},{3,2},{4,5},{5,4},{6,7},{7,6},{8,9},{9,8},{10,11... | collective-permute-start | bytes 417800 | tf_op jit(solution)/shard_map/ppermute | solution.py:414
  33.9 0.8 %collective-permute-start.6 = (f32[16,2048]{1,0:T(8,128)S(1)}, f32[16,2048]{1,0:T(8,128)S(1)}, u32[]{:S(2)}, u32[]{:S(2)}) collective-permute-start(f32[16,2048]{1,0:T(8,128)S(1)} %get-tuple-element.34), channel_id=1, source_target_pairs={{1,2},{3,4},{5,6},{7,8},{9,10},{11,12},{13,14},{2,1},{4,3},{6,5},{... | collective-permute-start | bytes 393224 | tf_op jit(solution)/shard_map/ppermute | solution.py:413
  34.8 0.8 %terms_inner.1.inner_part = f32[2,16,4096]{2,1,0:T(8,128)S(1)} custom-call(f32[32,8,128]{2,1,0:T(8,128)S(1)} %all_to_all.10.pieces_ref, bf16[2,2,128,8192]{3,2,1,0:T(8,128)(2,1)S(1)} %get-tuple-element.22.fields_ref, f32[2,32,64,256]{3,2,1,0:T(8,128)S(1)} %collective-permute-done.4.raw, f32[16,2176]{1,0:T(8,128)S(1)} %get-tuple-element.31._), custom_call_target="tpu_custom_call" | custom-call | flops 134217728 | tf_op jit(solution)/shard_map/terms_inner/pallas_call | solution.py:416
  35.6 1.9 %sketch.1 = (f32[16,8192]{1,0:T(8,128)S(1)}, f32[48,48]{1,0:T(8,128)S(1)}) custom-call(f32[2,16,4096]{2,1,0:T(8,128)S(1)} %terms_rim.1.own.rim_part, f32[2,16,4096]{2,1,0:T(8,128)S(1)} %terms_inner.1.inner_part, f32[32,256]{1,0:T(8,128)S(1)} %copy-done.4, f32[7,4,16,256]{3,2,1,0:T(8,128)S(1)} %get-tuple-element.32.saved), custom_call_target="tpu_custom_call" | custom-call | bytes 8388608 | tf_op jit(solution)/shard_map/sketch/pallas_call | solution.py:452
  37.5 0.0 collective-permute-done.6.other
  37.5 0.9 %collective-permute-done.5.pair = f32[16,2176]{1,0:T(8,128)S(1)} collective-permute-done((f32[16,2176]{1,0:T(8,128)S(1)}, f32[16,2176]{1,0:T(8,128)S(1)}, u32[]{:S(2)}, u32[]{:S(2)}) %collective-permute-start.5) | collective-permute-done | bytes 139296 | tf_op jit(solution)/shard_map/ppermute | solution.py:414
  38.4 0.5 gram.1
  39.0 0.1 collective-permute-start.7
  39.0 14.2 %all_to_all.11.grams = f32[32,8,128]{2,1,0:T(8,128)S(1)} all-to-all(f32[32,8,128]{2,1,0:T(8,128)S(1)} %get-tuple-element.36), channel_id=1, replica_groups=mesh['shot'=2,'strip'=16] {'shot','strip'}, dimensions={0} | all-to-all | bytes 262144 | tf_op jit(solution)/shard_map/all_to_all | solution.py:488
  53.2 0.0 collective-permute-done.7.theirs
  53.2 1.7 %factors.1 = (f32[16,32,256]{2,1,0:T(8,128)}, f32[16,32,256]{2,1,0:T(8,128)}) custom-call(f32[32,8,128]{2,1,0:T(8,128)S(1)} %all_to_all.11.grams, f32[16,8192]{1,0:T(8,128)S(1)} %get-tuple-element.37.own, f32[16,8192]{1,0:T(8,128)S(1)} %collective-permute-done.7.theirs), custom_call_target="tpu_custom_call" | custom-call | tf_op jit(solution)/shard_map/factors/pallas_call | solution.py:541
  (8 shorter events, 0.0 us)
Async XLA Ops:
  0.6 4.9 %copy-start.1 = (f32[1,64,32,256]{3,2,1,0:T(8,128)S(1)}, f32[1,64,32,256]{3,2,1,0:T(8,128)}, u32[]{:S(2)}) copy-start(f32[1,64,32,256]{3,2,1,0:T(8,128)} %param.10) | copy-start | bytes 6291460
  0.6 4.9 %copy-start = (f32[1,64,32,256]{3,2,1,0:T(8,128)S(1)}, f32[1,64,32,256]{3,2,1,0:T(8,128)}, u32[]{:S(2)}) copy-start(f32[1,64,32,256]{3,2,1,0:T(8,128)} %param.9) | copy-start | bytes 6291460
  0.7 4.9 %copy-start.3 = (f32[1,64,32,256]{3,2,1,0:T(8,128)S(1)}, f32[1,64,32,256]{3,2,1,0:T(8,128)}, u32[]{:S(2)}) copy-start(f32[1,64,32,256]{3,2,1,0:T(8,128)} %param.8) | copy-start | bytes 6291460
  0.7 4.9 %copy-start.2 = (f32[1,64,32,256]{3,2,1,0:T(8,128)S(1)}, f32[1,64,32,256]{3,2,1,0:T(8,128)}, u32[]{:S(2)}) copy-start(f32[1,64,32,256]{3,2,1,0:T(8,128)} %param.7) | copy-start | bytes 6291460
  1.9 8.7 %collective-permute-start = (f32[18,8,256]{2,1,0:T(8,128)S(1)}, f32[18,8,256]{2,1,0:T(8,128)S(1)}, u32[]{:S(2)}, u32[]{:S(2)}) collective-permute-start(f32[18,8,256]{2,1,0:T(8,128)S(1)} %get-tuple-element.20._), channel_id=1, source_target_pairs={{0,1},{1,0},{2,3},{3,2},{4,5},{5,4},{6,7},{7,6},{8,9},{9,8},{10,11... | collective-permute-start | bytes 442376 | tf_op jit(solution)/shard_map/ppermute | solution.py:147
  4.9 5.6 %collective-permute-start.1 = (f32[17,8,256]{2,1,0:T(8,128)S(1)}, f32[17,8,256]{2,1,0:T(8,128)S(1)}, u32[]{:S(2)}, u32[]{:S(2)}) collective-permute-start(f32[17,8,256]{2,1,0:T(8,128)S(1)} %get-tuple-element.25), channel_id=1, source_target_pairs={{1,2},{3,4},{5,6},{7,8},{9,10},{11,12},{13,14},{2,1},{4,3},{6,5},{... | collective-permute-start | bytes 417800 | tf_op jit(solution)/shard_map/ppermute | solution.py:146
  5.6 3.2 %copy-start.4 = (f32[32,256]{1,0:T(8,128)S(1)}, f32[32,256]{1,0:T(8,128)}, u32[]{:S(2)}) copy-start(f32[32,256]{1,0:T(8,128)} %speed.9) | copy-start | bytes 98308
  10.5 2.0 %collective-permute-start.3 = (f32[2,16,4096]{2,1,0:T(8,128)S(1)}, f32[2,16,4096]{2,1,0:T(8,128)S(1)}, u32[]{:S(2)}, u32[]{:S(2)}) collective-permute-start(f32[2,16,4096]{2,1,0:T(8,128)S(1)} %get-tuple-element.26.inner_mine), channel_id=1, source_target_pairs={{0,16},{16,0},{1,17},{17,1},{2,18},{18,2},{3,19},{19,3},{4,20},{20... | collective-permute-start | bytes 1572872 | tf_op jit(solution)/shard_map/ppermute | solution.py:243
  11.8 2.6 %collective-permute-start.2 = (f32[2,16,4096]{2,1,0:T(8,128)S(1)}, f32[2,16,4096]{2,1,0:T(8,128)S(1)}, u32[]{:S(2)}, u32[]{:S(2)}) collective-permute-start(f32[2,16,4096]{2,1,0:T(8,128)S(1)} %probes_rim.1.rim_mine), channel_id=1, source_target_pairs={{0,16},{16,0},{1,17},{17,1},{2,18},{18,2},{3,19},{19,3},{4,20},{20... | collective-permute-start | bytes 1572872 | tf_op jit(solution)/shard_map/ppermute | solution.py:289
  15.2 15.5 %collective-permute-start.4 = (f32[2,32,64,256]{3,2,1,0:T(8,128)S(1)}, f32[2,32,64,256]{3,2,1,0:T(8,128)S(1)}, u32[]{:S(2)}, u32[]{:S(2)}) collective-permute-start(f32[2,32,64,256]{3,2,1,0:T(8,128)S(1)} %get-tuple-element.30), channel_id=1, source_target_pairs={{0,16},{16,0},{1,17},{17,1},{2,18},{18,2},{3,19},{19,3},{4,20},{20... | collective-permute-start | bytes 12582920 | tf_op jit(solution)/shard_map/ppermute | solution.py:328
  32.7 5.7 %collective-permute-start.5 = (f32[16,2176]{1,0:T(8,128)S(1)}, f32[16,2176]{1,0:T(8,128)S(1)}, u32[]{:S(2)}, u32[]{:S(2)}) collective-permute-start(f32[16,2176]{1,0:T(8,128)S(1)} %get-tuple-element.31._), channel_id=1, source_target_pairs={{0,1},{1,0},{2,3},{3,2},{4,5},{5,4},{6,7},{7,6},{8,9},{9,8},{10,11... | collective-permute-start | bytes 417800 | tf_op jit(solution)/shard_map/ppermute | solution.py:414
  33.9 3.6 %collective-permute-start.6 = (f32[16,2048]{1,0:T(8,128)S(1)}, f32[16,2048]{1,0:T(8,128)S(1)}, u32[]{:S(2)}, u32[]{:S(2)}) collective-permute-start(f32[16,2048]{1,0:T(8,128)S(1)} %get-tuple-element.34), channel_id=1, source_target_pairs={{1,2},{3,4},{5,6},{7,8},{9,10},{11,12},{13,14},{2,1},{4,3},{6,5},{... | collective-permute-start | bytes 393224 | tf_op jit(solution)/shard_map/ppermute | solution.py:413
  39.0 14.2 %collective-permute-start.7 = (f32[16,8192]{1,0:T(8,128)S(1)}, f32[16,8192]{1,0:T(8,128)S(1)}, u32[]{:S(2)}, u32[]{:S(2)}) collective-permute-start(f32[16,8192]{1,0:T(8,128)S(1)} %get-tuple-element.37.own), channel_id=1, source_target_pairs={{0,16},{16,0},{1,17},{17,1},{2,18},{18,2},{3,19},{19,3},{4,20},{20... | collective-permute-start | bytes 1572872 | tf_op jit(solution)/shard_map/ppermute | solution.py:487
